TPU v7x, 512 devices: a whole 4x4x16 slice. The times are simulated.
512 devices in a mesh: section: 4 (over z_lo), dp: 16 (over z_hi, y), mp: 8 (over x, core).
Axes of the slice: x: 4, y: 4, z: 16 (z_hi: 4, z_lo: 4; z = z_hi * 4 + z_lo), core: 2. Of those that a mesh axis runs over, the one named last changes fastest.
Arguments:
- activations: bfloat16 [4, 80, 14, 14, 4096], P('section', 'dp', None, None, 'mp'), may hold values from -180 to 180
- conv_weight: bfloat16 [4, 4096, 2048], P('section', None, 'mp'), may hold values from -0.09375 to 0.09375
- norm_gain: float32 [4, 2048], P('section', 'mp'), may hold values from 0.5 to 2
- norm_bias: float32 [4, 2048], P('section', 'mp'), may hold values from -3 to 3
- cotangent: bfloat16 [4, 80, 7, 7, 2048], P('section', 'dp', None, None, 'mp'), may hold values from -60 to 60
Outputs:
- block_out: bfloat16 [4, 80, 7, 7, 2048], P('section', 'dp', None, None, 'mp')
- grad_input: bfloat16 [4, 80, 7, 7, 4096], P('section', 'dp', None, None, 'mp')
- grad_weight: bfloat16 [4, 4096, 2048], P('section', 'dp', 'mp')
- grad_gain: float32 [4, 2048], P('section', 'mp')
- grad_bias: float32 [4, 2048], P('section', 'mp')
All inputs are finite; a program needn't handle non-finite values.
Results may differ from a plain program's by a relative error of at most 0.023.
Values may be sent and summed in bfloat16 or wider, within the bound.
A program may use at most 64 MiB of HBM per device.

v0:
```python
import jax
import jax.numpy as jnp
from jax import lax
from jax.sharding import PartitionSpec as P


def from_partner(value, axis, apart):
    mask = 2**apart
    pairs = [(source, source ^ mask) for source in range(lax.axis_size(axis))]
    return lax.ppermute(value, axis, pairs)


def on_device(activations, conv_weight, norm_gain, norm_bias, cotangent):
    sampled = activations[0][:, ::2, ::2, :]
    complete = lax.all_gather(sampled, "mp", axis=3, tiled=True)
    arrived = from_partner(complete, "section", 0)
    images, height, img_width, channels = arrived.shape
    pixel_rows = arrived.reshape(images * height * img_width, channels)
    local_w = conv_weight[0]
    gain = norm_gain[0]
    shift_b = norm_bias[0]
    total_rows = pixel_rows.shape[0] * lax.axis_size("dp")
    hidden = jnp.dot(pixel_rows, local_w, preferred_element_type=jnp.float32)
    average = lax.psum(jnp.sum(hidden, axis=0), "dp") / total_rows
    centred = hidden - average
    spread = lax.psum(jnp.sum(centred * centred, axis=0), "dp") / total_rows
    inverse = lax.rsqrt(spread + 1e-05)
    normed = centred * inverse
    pre_act = gain * normed + shift_b
    squash = jax.nn.sigmoid(pre_act)
    block_out = (pre_act * squash).astype(jnp.bfloat16)
    grad_out = cotangent[0].reshape(pixel_rows.shape[0], -1).astype(jnp.float32)
    grad_pre = grad_out * squash * (1.0 + pre_act * (1.0 - squash))
    bias_grad, gain_grad = lax.psum(
        (jnp.sum(grad_pre, axis=0), jnp.sum(grad_pre * normed, axis=0)), "dp"
    )
    grad_hidden = (
        gain * inverse * (grad_pre - bias_grad / total_rows - normed * (gain_grad / total_rows))
    ).astype(jnp.bfloat16)
    weight_sum = lax.psum_scatter(
        lax.dot_general(
            pixel_rows, grad_hidden, (((0,), (0,)), ((), ())), preferred_element_type=jnp.float32
        ).astype(jnp.bfloat16),
        "dp",
        scatter_dimension=0,
        tiled=True,
    )
    grad_weight = weight_sum[None]
    input_term = lax.dot_general(
        grad_hidden, local_w, (((1,), (1,)), ((), ())), preferred_element_type=jnp.float32
    )
    input_share = lax.psum_scatter(
        input_term.astype(jnp.bfloat16), "mp", scatter_dimension=1, tiled=True
    )
    returned = from_partner(input_share, "section", 0)
    grad_input = returned.reshape(1, images, height, img_width, -1)
    return (
        block_out.reshape(1, images, height, img_width, -1),
        grad_input,
        grad_weight,
        gain_grad[None],
        bias_grad[None],
    )


def solution(mesh):
    placed = (
        P("section", "dp", None, None, "mp"),
        P("section", None, "mp"),
        P("section", "mp"),
        P("section", "mp"),
        P("section", "dp", None, None, "mp"),
    )
    return jax.shard_map(
        on_device,
        mesh=mesh,
        in_specs=placed,
        out_specs=(
            P("section", "dp", None, None, "mp"),
            P("section", "dp", None, None, "mp"),
            P("section", "dp", "mp"),
            P("section", "mp"),
            P("section", "mp"),
        ),
        check_vma=False,
    )
```

profile of v0, /device:TPU:6, one launch (start us, length us, event | category | flops | bytes accessed | tf_op | source)
XLA Modules:
  0.0 447.1 jit_solution(3348440970601962431)
XLA Ops:
  7.2 0.0 copy-start
  7.2 0.0 all-gather.2.cloned.1.call-start
  7.2 16.8 %slice.3 = bf16[5,7,7,512]{3,2,1,0:T(8,128)(2,1)} slice(bf16[5,14,14,512]{3,2,1,0:T(8,128)(2,1)} %bitcast.20), slice={[0:5:1], [0:14:2], [0:14:2], [0:512:1]} | slice | bytes 501760 | tf_op jit(solution)/shard_map/slice | solution.py:14
  24.0 0.0 all-gather.2.cloned.1.call-update
  24.1 0.0 reduce-scatter.3.cloned.1.call-start
  24.1 36.6 %all-gather.2.cloned.1.call-done = bf16[5,7,7,4096]{3,2,1,0:T(8,128)(2,1)} async-done(((bf16[5,7,7,512]{3,2,1,0:T(8,128)(2,1)}), bf16[5,7,7,4096]{3,2,1,0:T(8,128)(2,1)}) %all-gather.2.cloned.1.call-update) | async-done | bytes 2007056 | tf_op jit(solution)/shard_map/all_gather | solution.py:15
  60.7 3.5 collective-permute-start
  64.2 1.0 reshape.29
  65.1 49.8 %collective-permute-done = bf16[5,7,7,4096]{3,2,1,0:T(8,128)(2,1)} collective-permute-done((bf16[5,7,7,4096]{3,2,1,0:T(8,128)(2,1)}, bf16[5,7,7,4096]{3,2,1,0:T(8,128)(2,1)}, u32[]{:S(2)}, u32[]{:S(2)}) %collective-permute-start) | collective-permute-done | bytes 2007072 | tf_op jit(solution)/shard_map/ppermute | solution.py:10
  114.9 3.5 reshape.26
  118.4 0.0 copy-done
  118.4 0.0 copy-start.1
  118.4 0.0 copy-start.2
  118.4 2.3 fusion.6
  120.7 54.9 %psum.28 = f32[256]{0:T(256)S(1)} all-reduce(f32[256]{0:T(256)S(1)} %get-tuple-element.18), channel_id=1, replica_groups=mesh['section'=4,'dp'=16,'mp'=8] {'dp'}, use_global_device_ids=true, to_apply=%region_1.0 | all-reduce | flops 256 | bytes 2048 | tf_op jit(solution)/shard_map/psum | solution.py:24
  175.6 0.1 multiply_reduce_fusion.1
  175.7 46.3 %psum.29 = f32[256]{0:T(256)S(1)} all-reduce(f32[256]{0:T(256)S(1)} %multiply_reduce_fusion.1), channel_id=1, replica_groups=mesh['section'=4,'dp'=16,'mp'=8] {'dp'}, use_global_device_ids=true, to_apply=%region_3.0 | all-reduce | flops 256 | bytes 2048 | tf_op jit(solution)/shard_map/psum | solution.py:26
  222.0 0.0 copy-done.1
  222.0 0.0 copy-done.2
  222.0 0.2 fusion.5
  222.2 48.3 %all-reduce = (f32[256]{0:T(256)S(1)}, f32[256]{0:T(256)S(1)}) all-reduce(f32[256]{0:T(256)S(1)} %get-tuple-element.11, f32[256]{0:T(256)S(1)} %get-tuple-element.10), channel_id=1, replica_groups=mesh['section'=4,'dp'=16,'mp'=8] {'dp'}, use_global_device_ids=true, to_apply=%region_7.0 | all-reduce | flops 512 | bytes 4096 | tf_op jit(solution)/shard_map/psum | solution.py:34
  270.5 0.0 copy-start.3
  270.5 0.0 copy-start.4
  270.5 0.1 multiply_convert_fusion
  270.6 2.0 convolution_convert_fusion.1
  272.6 0.0 copy-done.3
  272.6 0.0 copy-done.4
  272.6 0.0 reduce-scatter.3.cloned.1.call-update
  272.6 0.0 reduce-scatter.5.cloned.1.call-start
  272.7 3.6 fusion
  276.3 0.0 reduce-scatter.5.cloned.1.call-update
  276.4 27.9 %reduce-scatter.3.cloned.1.call-done = bf16[245,512]{1,0:T(8,128)(2,1)} async-done(((bf16[245,4096]{1,0:T(8,128)(2,1)}), bf16[245,512]{1,0:T(8,128)(2,1)}) %reduce-scatter.3.cloned.1.call-update) | async-done | bytes 250896 | tf_op jit(solution)/shard_map/reduce_scatter | solution.py:52
  304.3 3.5 collective-permute-start.1
  307.8 0.7 reshape.27
  308.5 129.6 %reduce-scatter.5.cloned.1.call-done = bf16[256,256]{0,1:T(8,128)(2,1)} async-done(((bf16[4096,256]{0,1:T(8,128)(2,1)}), bf16[256,256]{0,1:T(8,128)(2,1)}) %reduce-scatter.5.cloned.1.call-update) | async-done | bytes 131088 | tf_op jit(solution)/shard_map/reduce_scatter | solution.py:40
  438.1 1.7 copy.10
  439.7 0.0 collective-permute-done.1
  439.7 0.8 reshape.28
  (3 shorter events, 0.0 us)
Async XLA Ops:
  7.2 111.2 %copy-start = (bf16[1,4096,256]{2,1,0:T(8,128)(2,1)S(1)}, bf16[1,4096,256]{2,1,0:T(8,128)(2,1)}, u32[]{:S(2)}) copy-start(bf16[1,4096,256]{2,1,0:T(8,128)(2,1)} %param.6) | copy-start | bytes 6291460
  7.2 53.5 %all-gather.2.cloned.1.call-start = ((), (), s32[]{:S(2)}) async-start(), calls=%async_computation.2 | async-start | bytes 2580480 | tf_op jit(solution)/shard_map/all_gather | solution.py:15
  24.1 280.2 %reduce-scatter.3.cloned.1.call-start = ((), (), s32[]{:S(2)}) async-start(), calls=%async_computation.3 | async-start | bytes 2285568 | tf_op jit(solution)/shard_map/reduce_scatter | solution.py:52
  60.7 54.2 %collective-permute-start = (bf16[5,7,7,4096]{3,2,1,0:T(8,128)(2,1)}, bf16[5,7,7,4096]{3,2,1,0:T(8,128)(2,1)}, u32[]{:S(2)}, u32[]{:S(2)}) collective-permute-start(bf16[5,7,7,4096]{3,2,1,0:T(8,128)(2,1)} %all-gather.2.cloned.1.call-done), channel_id=1, source_target_pairs={{0,128},{128,0},{256,384},{384,256},{1,129},{129,1},{257,385},{385... | collective-permute-start | bytes 6021128 | tf_op jit(solution)/shard_map/ppermute | solution.py:10
  118.4 103.6 %copy-start.1 = (f32[1,256]{1,0:T(1,128)S(1)}, f32[1,256]{1,0:T(1,128)}, u32[]{:S(2)}) copy-start(f32[1,256]{1,0:T(1,128)} %param.7) | copy-start | bytes 3076
  118.4 103.6 %copy-start.2 = (f32[1,256]{1,0:T(1,128)S(1)}, f32[1,256]{1,0:T(1,128)}, u32[]{:S(2)}) copy-start(f32[1,256]{1,0:T(1,128)} %param.8) | copy-start | bytes 3076
  270.5 2.1 copy-start.3
  270.5 2.1 copy-start.4
  272.6 165.4 %reduce-scatter.5.cloned.1.call-start = ((), (), s32[]{:S(2)}) async-start(), calls=%async_computation.4 | async-start | bytes 2228224 | tf_op jit(solution)/shard_map/reduce_scatter | solution.py:40
  304.3 135.5 %collective-permute-start.1 = (bf16[245,512]{1,0:T(8,128)(2,1)}, bf16[245,512]{1,0:T(8,128)(2,1)S(1)}, u32[]{:S(2)}, u32[]{:S(2)}) collective-permute-start(bf16[245,512]{1,0:T(8,128)(2,1)} %reduce-scatter.3.cloned.1.call-done), channel_id=1, source_target_pairs={{0,128},{128,0},{256,384},{384,256},{1,129},{129,1},{257,385},{385... | collective-permute-start | bytes 752648 | tf_op jit(solution)/shard_map/ppermute | solution.py:10
Sparse Core Ops, SparseCore 0:
  24.2 36.4 all-gather.1
  272.8 31.4 reduce-scatter.2
  309.0 129.0 reduce-scatter.4
where the time goes:
time: 449 us; the launch traced here: 447 us
  waiting for transfers between devices  244 us (54%)
  blocking collectives  150 us (33%)
  local copies, waits for them, and re-layouts  24.5 us (5%)
  between operations  13.8 us (3%)
  matrix products  7.98 us (2%)
  starting transfers between devices  7.08 us (2%)
    reduce_scatter x1, waiting for transfers between devices, on_device(): lax.psum_scatter(lax.dot_general(pixel_rows, grad_hidden, (((0,), (0,)),...  130 us
    psum x1, blocking collectives, on_device(): average = lax.psum(jnp.sum(hidden, axis=0), 'dp') / total_rows  54.9 us
    ppermute x2, waiting for transfers between devices, from_partner(): return lax.ppermute(value, axis, pairs)  49.8 us
    psum x1, blocking collectives, on_device(): lax.psum((jnp.sum(grad_pre, axis=0), jnp.sum(grad_pre * normed, axis=0)),...  48.3 us
    psum x1, blocking collectives, on_device(): spread = lax.psum(jnp.sum(centred * centred, axis=0), 'dp') / total_rows  46.3 us
    all_gather x1, waiting for transfers between devices, on_device(): complete = lax.all_gather(sampled, 'mp', axis=3, tiled=True)  36.6 us
    reduce_scatter x1, waiting for transfers between devices, on_device(): lax.psum_scatter(input_term.astype(jnp.bfloat16), 'mp', scatter_dimension...  27.9 us
    slice x1, local copies, waits for them, and re-layouts, on_device(): sampled = activations[0][:, ::2, ::2, :]  16.8 us
  transfers between devices with their start and end apart: 5, of which 4 were waited for; matrix products, arithmetic and copies ran while one was open for 2% of the time, Pallas kernels for 0%

commit v1 on v0

v1 whole, which is shorter than its diff:
```python
import functools

import jax
import jax.numpy as jnp
from jax import lax
from jax.experimental import pallas as pl
from jax.experimental.pallas import tpu as pltpu
from jax.sharding import PartitionSpec as P

BF16 = jnp.bfloat16
F32 = jnp.float32
RING = 4
ROWS = 245
PAD = 256
HALF = PAD // 2
CH = 512
COLS = 256
TILE = 16
STRIPS = 35
COPIES = 64


def dot(a, b, over):
    return lax.dot_general(a, b, ((over[:1], over[1:]), ((), ())), preferred_element_type=F32)


def picks(step):
    shape = (PAD, STRIPS * TILE)
    row = lax.broadcasted_iota(jnp.int32, shape, 0)
    col = lax.broadcasted_iota(jnp.int32, shape, 1)
    pixel = col & (TILE - 1)
    wanted = 7 * (col >> 4) + (pixel if step == 1 else pixel >> 1)
    keep = (row == wanted) & (pixel < 7 * step)
    if step == 2:
        keep = keep & ((pixel & 1) == 0)
    return jnp.where(keep, 1.0, 0.0).astype(F32).astype(BF16)


def kernel(
    acts, weight, gain_ref, shift_ref, cotan,
    block_out, grad_input, grad_weight, gain_grad, bias_grad,
    raw, strips, w, ct_raw, ct_strips, own, full, ex, gh, hid,
    ys, zs, yg, zg,
    to_sib, from_sib, xb, x_opp, x_left, x_right,
    zb, z_opp, z_left, z_right, share, returned,
    send_sems, recv_sems, local_sems,
):
    section, dp, mp = lax.axis_index("section"), lax.axis_index("dp"), lax.axis_index("mp")
    zh, y = lax.div(dp, RING), lax.rem(dp, RING)
    x, core = lax.div(mp, 2), lax.rem(mp, 2)

    def around(at, by):
        return lax.rem(at + by, RING)

    partner = {"section": section + 1 - 2 * lax.rem(section, 2)}
    sibling = {"mp": 2 * x + 1 - core}
    at_x = [{"mp": 2 * around(x, o) + core} for o in range(RING)]
    at_y = [{"dp": RING * zh + around(y, o)} for o in range(RING)]
    at_z = [{"dp": RING * around(zh, o) + y} for o in range(RING)]
    peers = [partner, sibling, at_x[1], at_x[3]] + at_y[1:] + at_z[1:]

    started = []
    ids = iter(range(COPIES))

    def names(n):
        return [next(ids) for _ in range(n)]

    def send(src, dst, k, to):
        copy = pltpu.make_async_remote_copy(
            src_ref=src, dst_ref=dst, send_sem=send_sems.at[k], recv_sem=recv_sems.at[k],
            device_id=to, device_id_type=pl.DeviceIdType.MESH,
        )
        copy.start()
        started.append(copy)

    def arrive(dst, k):
        pltpu.make_async_remote_copy(
            src_ref=dst, dst_ref=dst, send_sem=send_sems.at[k], recv_sem=recv_sems.at[k],
            device_id=sibling, device_id_type=pl.DeviceIdType.MESH,
        ).wait_recv()

    load_acts = pltpu.make_async_copy(acts.at[:, :, 0], raw, local_sems.at[0])
    load_w = pltpu.make_async_copy(weight, w, local_sems.at[1])
    load_ct = pltpu.make_async_copy(cotan, ct_raw, local_sems.at[2])
    load_acts.start()
    load_w.start()
    load_ct.start()
    barrier = pltpu.get_barrier_semaphore()
    for peer in peers:
        pl.semaphore_signal(barrier, inc=1, device_id=peer, device_id_type=pl.DeviceIdType.MESH)
    strips[...] = jnp.zeros_like(strips)
    ct_strips[...] = jnp.zeros_like(ct_strips)
    load_acts.wait()
    strips[:, 0:14, :] = raw[...].reshape(STRIPS, 14, CH)
    own[...] = dot(picks(2), strips[...].reshape(STRIPS * TILE, CH), (1, 0)).astype(BF16)
    pl.semaphore_wait(barrier, len(peers))

    halves = [pl.ds(0, HALF), pl.ds(HALF, HALF)]
    k_part, k_left, k_right, k_sib = names(2), names(2), names(2), names(2)
    k_sl, k_sr, k_so, k_opp = names(2), names(2), names(2), names(2)
    for h in range(2):
        send(own.at[halves[h]], full.at[x, core, halves[h]], k_part[h], partner)
    for h in range(2):
        mine = full.at[x, core, halves[h]]
        arrive(mine, k_part[h])
        send(mine, mine, k_right[h], at_x[1])
        send(mine, mine, k_left[h], at_x[3])
        send(mine, mine, k_sib[h], sibling)
    load_ct.wait()
    ct_strips[:, 0:7, :] = ct_raw[...].reshape(STRIPS, 7, COLS)
    grad_out = dot(picks(1), ct_strips[...].reshape(STRIPS * TILE, COLS), (1, 0))
    load_w.wait()

    def w_block(xx, cc):
        return w[pl.ds(pl.multiple_of(CH * (2 * xx + cc), CH), CH), :]

    def term(xx, cc):
        return dot(full[xx, cc], w_block(xx, cc), (1, 0))

    lx, rx, ox = around(x, 3), around(x, 1), around(x, 2)
    for h in range(2):
        from_left = full.at[lx, core, halves[h]]
        arrive(from_left, k_right[h])
        if h == 0:
            send(from_left, from_left, k_opp[0], at_x[1])
        send(from_left, from_left, k_sl[h], sibling)
        from_right = full.at[rx, core, halves[h]]
        arrive(from_right, k_left[h])
        if h == 1:
            send(from_right, from_right, k_opp[1], at_x[3])
        send(from_right, from_right, k_sr[h], sibling)
    hid[...] = term(x, core)
    for h in range(2):
        arrive(full.at[x, 1 - core, halves[h]], k_sib[h])
    hid[...] += term(x, 1 - core)
    hid[...] += term(lx, core)
    hid[...] += term(rx, core)
    for h in range(2):
        arrive(full.at[lx, 1 - core, halves[h]], k_sl[h])
    hid[...] += term(lx, 1 - core)
    for h in range(2):
        arrive(full.at[rx, 1 - core, halves[h]], k_sr[h])
    hid[...] += term(rx, 1 - core)
    for h in range(2):
        opposite = full.at[ox, core, halves[h]]
        arrive(opposite, k_opp[h])
        send(opposite, opposite, k_so[h], sibling)
    hid[...] += term(ox, core)
    for h in range(2):
        arrive(full.at[ox, 1 - core, halves[h]], k_so[h])
    hid[...] += term(ox, 1 - core)
    hidden = hid[...]

    def spread_out(buf, me, to, value, ks):
        buf[me] = value
        for o in range(1, RING):
            send(buf.at[me], buf.at[me], ks[o - 1], to[o])

    def collect(buf, me, ks):
        for o in range(1, RING):
            arrive(buf.at[around(me, RING - o)], ks[o - 1])

    def two_rows(a, b):
        row = lax.broadcasted_iota(jnp.int32, (8, COLS), 0)
        return jnp.where(row == 0, a, jnp.where(row == 1, b, 0.0))

    def merge(buf, count):
        means = [buf[i, 0:1, :] for i in range(RING)]
        squares = [buf[i, 1:2, :] for i in range(RING)]
        mean = sum(means) / RING
        return mean, sum(squares) + count * sum((m - mean) * (m - mean) for m in means)

    valid = lax.broadcasted_iota(jnp.int32, (PAD, COLS), 0) < ROWS
    mean = jnp.sum(hidden, axis=0, keepdims=True) / ROWS
    off = jnp.where(valid, hidden - mean, 0.0)
    square = jnp.sum(off * off, axis=0, keepdims=True)
    k_ys, k_zs, k_yg, k_zg = names(3), names(3), names(3), names(3)
    spread_out(ys, y, at_y, two_rows(mean, square), k_ys)

    k_ex, k_es = names(3), names(3)

    def quarter(yy, rows):
        at = pl.multiple_of(COLS * lax.rem(yy, 2), COLS)
        return full.at[:, lax.div(yy, 2), rows, pl.ds(at, COLS)]

    def ex_rows(yy, cc):
        return ex.at[:, pl.ds(pl.multiple_of(PAD * yy + HALF * cc, HALF), HALF), :]

    my_rows = pl.ds(pl.multiple_of(HALF * core, HALF), HALF)
    for o in (2, 1, 3):
        send(quarter(around(y, o), my_rows), ex_rows(y, core), k_ex[o - 1], at_y[o])
    keep = pltpu.make_async_copy(
        quarter(y, pl.ds(0, PAD)),
        ex.at[:, pl.ds(pl.multiple_of(PAD * y, PAD), PAD), :],
        local_sems.at[3],
    )
    keep.start()

    collect(ys, y, k_ys)
    mean, square = merge(ys, float(ROWS))
    spread_out(zs, zh, at_z, two_rows(mean, square), k_zs)
    collect(zs, zh, k_zs)
    mean, square = merge(zs, float(ROWS * RING))
    total = float(ROWS * RING * RING)
    inverse = lax.rsqrt(square / total + 1e-05)
    gain, shift = gain_ref[...], shift_ref[...]
    normed = (hidden - mean) * inverse
    pre_act = gain * normed + shift
    squash = jax.nn.sigmoid(pre_act)
    grad_pre = grad_out * squash * (1.0 + pre_act * (1.0 - squash))
    d_bias = jnp.sum(grad_pre, axis=0, keepdims=True)
    d_gain = jnp.sum(grad_pre * normed, axis=0, keepdims=True)
    spread_out(yg, y, at_y, two_rows(d_bias, d_gain), k_yg)
    spaced = dot(picks(1), (pre_act * squash).astype(BF16), (0, 0)).reshape(STRIPS, TILE, COLS)
    block_out[...] = spaced[:, 0:7, :].astype(BF16)
    collect(yg, y, k_yg)
    spread_out(zg, zh, at_z, yg[0] + yg[1] + yg[2] + yg[3], k_zg)
    collect(zg, zh, k_zg)
    sums = zg[0] + zg[1] + zg[2] + zg[3]
    d_bias, d_gain = sums[0:1, :], sums[1:2, :]
    bias_grad[...] = d_bias
    gain_grad[...] = d_gain
    grad_hidden = (
        gain * inverse * (grad_pre - d_bias / total - normed * (d_gain / total))
    ).astype(BF16)

    k_up, k_down, k_far = names(2), names(2), names(2)

    def gh_rows(yy, h):
        return gh.at[pl.ds(pl.multiple_of(PAD * yy + HALF * h, HALF), HALF), :]

    gh[pl.ds(pl.multiple_of(PAD * y, PAD), PAD), :] = grad_hidden
    for h in range(2):
        send(gh_rows(y, h), gh_rows(y, h), k_up[h], at_y[1])
        send(gh_rows(y, h), gh_rows(y, h), k_down[h], at_y[3])

    k_cs = names(4)
    order = (2, 1, 3, 0)
    for o in order:
        to_sib[o] = dot(grad_hidden, w_block(around(x, o), 1 - core), (1, 1)).astype(BF16)
        send(to_sib.at[o], from_sib.at[o], k_cs[o], sibling)

    for o in (1, 3, 2):
        yy = around(y, RING - o)
        arrive(ex_rows(yy, core), k_ex[o - 1])
        send(ex_rows(yy, core), ex_rows(yy, core), k_es[o - 1], sibling)

    ly, ry, oy = around(y, 3), around(y, 1), around(y, 2)
    arrive(gh_rows(ly, 0), k_up[0])
    send(gh_rows(ly, 0), gh_rows(ly, 0), k_far[0], at_y[1])
    arrive(gh_rows(ry, 0), k_down[0])
    arrive(gh_rows(ry, 1), k_down[1])
    send(gh_rows(ry, 1), gh_rows(ry, 1), k_far[1], at_y[3])
    arrive(gh_rows(ly, 1), k_up[1])

    def ring_start(block, opp, left, right, to, ks):
        send(block.at[2, halves[0]], opp.at[0], ks[0], to[1])
        send(block.at[2, halves[1]], opp.at[1], ks[1], to[3])
        send(block.at[1, halves[1]], left.at[1], ks[2], to[1])
        send(block.at[3, halves[0]], right.at[0], ks[3], to[3])

    def ring_middle(block, opp, left, right, to, ks):
        arrive(opp.at[0], ks[0])
        block[1, halves[0]] = (block[1, halves[0]].astype(F32) + opp[0].astype(F32)).astype(BF16)
        send(block.at[1, halves[0]], left.at[0], ks[4], to[1])
        arrive(opp.at[1], ks[1])
        block[3, halves[1]] = (block[3, halves[1]].astype(F32) + opp[1].astype(F32)).astype(BF16)
        send(block.at[3, halves[1]], right.at[1], ks[5], to[3])

    def ring_end(block, left, right, ks):
        arrive(left.at[1], ks[2])
        arrive(right.at[0], ks[3])
        arrive(left.at[0], ks[4])
        arrive(right.at[1], ks[5])
        out = []
        for h in range(2):
            out.append(
                block[0, halves[h]].astype(F32) + left[h].astype(F32) + right[h].astype(F32)
            )
        return [part.astype(BF16) for part in out]

    k_x, k_z, k_back = names(6), names(6), names(1)
    for o in order:
        part = dot(grad_hidden, w_block(around(x, o), core), (1, 1))
        arrive(from_sib.at[o], k_cs[o])
        xb[o] = (part + from_sib[o].astype(F32)).astype(BF16)
    ring_start(xb, x_opp, x_left, x_right, at_x, k_x)

    arrive(gh_rows(oy, 0), k_far[0])
    arrive(gh_rows(oy, 1), k_far[1])
    keep.wait()
    for o in (1, 3, 2):
        yy = around(y, RING - o)
        arrive(ex_rows(yy, 1 - core), k_es[o - 1])
    for o in order:
        zb[o] = dot(ex[around(zh, o)], gh[...], (0, 0)).astype(BF16)
    ring_start(zb, z_opp, z_left, z_right, at_z, k_z)

    ring_middle(xb, x_opp, x_left, x_right, at_x, k_x)
    halves_x = ring_end(xb, x_left, x_right, k_x)
    for h in range(2):
        share[halves[h], :] = halves_x[h]
    send(share, returned, k_back[0], partner)

    ring_middle(zb, z_opp, z_left, z_right, at_z, k_z)
    arrive(returned, k_back[0])
    spaced = dot(picks(1), returned[...], (0, 0)).reshape(STRIPS, TILE, CH)
    grad_input[...] = spaced[:, 0:7, :].astype(BF16)

    halves_z = ring_end(zb, z_left, z_right, k_z)
    for h in range(2):
        grad_weight[halves[h], :] = halves_z[h]
    for copy in started:
        copy.wait_send()


def on_device(activations, conv_weight, norm_gain, norm_bias, cotangent):
    images = activations.shape[1]
    acts = activations.reshape(images, 7, 2, 14, CH)
    cotan = cotangent.reshape(images, 7, 7, COLS)
    hbm = pl.BlockSpec(memory_space=pl.ANY)
    vmem = pl.BlockSpec(memory_space=pltpu.VMEM)
    block_out, grad_input, grad_weight, gain_grad, bias_grad = pl.pallas_call(
        kernel,
        out_shape=(
            jax.ShapeDtypeStruct((STRIPS, 7, COLS), BF16),
            jax.ShapeDtypeStruct((STRIPS, 7, CH), BF16),
            jax.ShapeDtypeStruct((COLS, COLS), BF16),
            jax.ShapeDtypeStruct((1, COLS), F32),
            jax.ShapeDtypeStruct((1, COLS), F32),
        ),
        in_specs=[hbm, hbm, vmem, vmem, hbm],
        out_specs=[vmem] * 5,
        scratch_shapes=[
            pltpu.VMEM((images, 7, 14, CH), BF16),
            pltpu.VMEM((STRIPS, TILE, CH), BF16),
            pltpu.VMEM((RING * 2 * CH, COLS), BF16),
            pltpu.VMEM((images, 7, 7, COLS), BF16),
            pltpu.VMEM((STRIPS, TILE, COLS), BF16),
            pltpu.VMEM((PAD, CH), BF16),
            pltpu.VMEM((RING, 2, PAD, CH), BF16),
            pltpu.VMEM((RING, RING * PAD, COLS), BF16),
            pltpu.VMEM((RING * PAD, COLS), BF16),
            pltpu.VMEM((PAD, COLS), F32),
            pltpu.VMEM((RING, 8, COLS), F32),
            pltpu.VMEM((RING, 8, COLS), F32),
            pltpu.VMEM((RING, 8, COLS), F32),
            pltpu.VMEM((RING, 8, COLS), F32),
            pltpu.VMEM((RING, PAD, CH), BF16),
            pltpu.VMEM((RING, PAD, CH), BF16),
            pltpu.VMEM((RING, PAD, CH), BF16),
            pltpu.VMEM((2, HALF, CH), BF16),
            pltpu.VMEM((2, HALF, CH), BF16),
            pltpu.VMEM((2, HALF, CH), BF16),
            pltpu.VMEM((RING, PAD, COLS), BF16),
            pltpu.VMEM((2, HALF, COLS), BF16),
            pltpu.VMEM((2, HALF, COLS), BF16),
            pltpu.VMEM((2, HALF, COLS), BF16),
            pltpu.VMEM((PAD, CH), BF16),
            pltpu.VMEM((PAD, CH), BF16),
            pltpu.SemaphoreType.DMA((COPIES,)),
            pltpu.SemaphoreType.DMA((COPIES,)),
            pltpu.SemaphoreType.DMA((4,)),
        ],
        compiler_params=pltpu.CompilerParams(
            collective_id=0, has_side_effects=True, vmem_limit_bytes=48 * 2**20
        ),
        name="bottleneck",
    )(acts, conv_weight[0], norm_gain, norm_bias, cotan)
    return (
        block_out.reshape(1, images, 7, 7, COLS),
        grad_input.reshape(1, images, 7, 7, CH),
        grad_weight[None],
        gain_grad,
        bias_grad,
    )


def solution(mesh):
    placed = (
        P("section", "dp", None, None, "mp"),
        P("section", None, "mp"),
        P("section", "mp"),
        P("section", "mp"),
        P("section", "dp", None, None, "mp"),
    )
    return jax.shard_map(
        on_device,
        mesh=mesh,
        in_specs=placed,
        out_specs=(
            P("section", "dp", None, None, "mp"),
            P("section", "dp", None, None, "mp"),
            P("section", "dp", "mp"),
            P("section", "mp"),
            P("section", "mp"),
        ),
        check_vma=False,
    )
```

time: 449 us -> 103 us (0.23)
  waiting for transfers between devices: 244 us -> 0 us
  blocking collectives: 150 us -> 0 us
  Pallas kernels: 0 us -> 93.4 us
  local copies, waits for them, and re-layouts: 24.5 us -> 8.26 us
  between operations: 13.8 us -> 0.66 us
  matrix products: 7.98 us -> 0 us
  starting transfers between devices: 7.08 us -> 0 us
    reduce_scatter x2 -> x0, waiting for transfers between devices: 157 us -> none  [the longest x1 130 us: on_device(): lax.psum_scatter(lax.dot_general(pixel_rows, grad_hidden, (((0,), (0,)),...]
    psum x3 -> x0, blocking collectives: 150 us -> none  [the longest x1 54.9 us: on_device(): average = lax.psum(jnp.sum(hidden, axis=0), 'dp') / total_rows]
    pallas_call x0 -> x1, Pallas kernels: none -> 93.4 us  [on_device(): pl.pallas_call(kernel, out_shape=(jax.ShapeDtypeStruct((STRIPS, 7, COLS),...]
    ppermute x2 -> x0, waiting for transfers between devices: 49.8 us -> none  [from_partner(): return lax.ppermute(value, axis, pairs)]
    all_gather x1 -> x0, waiting for transfers between devices: 36.6 us -> none  [on_device(): complete = lax.all_gather(sampled, 'mp', axis=3, tiled=True)]
    slice x1 -> x0, local copies, waits for them, and re-layouts: 16.8 us -> none  [on_device(): sampled = activations[0][:, ::2, ::2, :]]
    dot_general x3 -> x0, matrix products: 7.98 us -> none  [the longest x1 3.65 us: on_device(): lax.dot_general(pixel_rows, grad_hidden, (((0,), (0,)), ((), ())), prefer...]
    ppermute x2 -> x0, starting transfers between devices: 6.96 us -> none  [from_partner(): return lax.ppermute(value, axis, pairs)]
  transfers between devices with their start and end apart: 5 -> 0, of which waited for: 4 -> 0; matrix products, arithmetic and copies ran while one was open for 2% -> 0% of each run, Pallas kernels for 0% -> 0%
where the time goes in v1:
time: 103 us; the launch traced here: 102 us
  Pallas kernels  93.4 us (91%)
  local copies, waits for them, and re-layouts  8.26 us (8%)
    pallas_call x1, Pallas kernels, on_device(): pl.pallas_call(kernel, out_shape=(jax.ShapeDtypeStruct((STRIPS, 7, COLS),...  93.4 us
    unnamed x15, local copies, waits for them, and re-layouts  8.26 us

profile of v1, /device:TPU:6, one launch (start us, length us, event | category | flops | bytes accessed | tf_op | source)
XLA Modules:
  0.0 102.4 jit_solution(6227820501711556908)
XLA Ops:
  0.6 0.0 copy-start
  0.6 1.6 %copy-done = bf16[1,4096,256]{2,1,0:T(8,128)(2,1)S(1)} copy-done((bf16[1,4096,256]{2,1,0:T(8,128)(2,1)S(1)}, bf16[1,4096,256]{2,1,0:T(8,128)(2,1)}, u32[]{:S(2)}) %copy-start) | copy-done | bytes 2097176
  2.2 0.0 copy-start.1
  2.2 1.3 %copy-done.1 = bf16[1,5,14,14,512]{4,3,2,1,0:T(8,128)(2,1)S(1)} copy-done((bf16[1,5,14,14,512]{4,3,2,1,0:T(8,128)(2,1)S(1)}, bf16[1,5,14,14,512]{4,3,2,1,0:T(8,128)(2,1)}, u32[]{:S(2)}) %copy-start.1) | copy-done | bytes 1003544
  3.5 0.0 copy-start.2
  3.5 0.9 copy-done.2
  4.4 0.0 copy-start.3
  4.4 0.7 copy-done.3
  5.1 0.0 copy-start.4
  5.1 0.7 copy-done.4
  5.8 93.4 %bottleneck.1 = (bf16[35,7,256]{2,1,0:T(8,128)(2,1)S(1)}, bf16[35,7,512]{2,1,0:T(8,128)(2,1)S(1)}, bf16[256,256]{1,0:T(8,128)(2,1)S(1)}, f32[1,256]{1,0:T(1,128)S(1)}, f32[1,256]{1,0:T(1,128)S(1)}) custom-call(bf16[5,7,2,14,512]{4,3,2,1,0:T(8,128)(2,1)S(1)} %bitcast.7, bf16[4096,256]{1,0:T(8,128)(2,1)S(1)} %bitcast.6, f32[1,256]{1,0:T(1,128)S(1)} %copy-done.3, ...), custom_call_target="tpu_custom_call" | custom-call | tf_op jit(solution)/shard_map/bottleneck/pallas_call | solution.py:323
  99.2 0.7 copy.15
  99.9 0.7 copy.16
  100.6 0.7 copy.17
  101.2 0.6 copy.18
  101.8 0.6 copy.19
Async XLA Ops:
  0.6 1.6 %copy-start = (bf16[1,4096,256]{2,1,0:T(8,128)(2,1)S(1)}, bf16[1,4096,256]{2,1,0:T(8,128)(2,1)}, u32[]{:S(2)}) copy-start(bf16[1,4096,256]{2,1,0:T(8,128)(2,1)} %param.6) | copy-start | bytes 6291460
  2.2 1.3 %copy-start.1 = (bf16[1,5,14,14,512]{4,3,2,1,0:T(8,128)(2,1)S(1)}, bf16[1,5,14,14,512]{4,3,2,1,0:T(8,128)(2,1)}, u32[]{:S(2)}) copy-start(bf16[1,5,14,14,512]{4,3,2,1,0:T(8,128)(2,1)} %param.5) | copy-start | bytes 3010564
  3.5 0.9 copy-start.2
  4.4 0.7 copy-start.3
  5.1 0.7 copy-start.4

commit v2 on v0

v2 whole, which is shorter than its diff:
```python
import functools

import jax
import jax.numpy as jnp
from jax import lax
from jax.experimental import pallas as pl
from jax.experimental.pallas import tpu as pltpu
from jax.sharding import PartitionSpec as P

BF16 = jnp.bfloat16
F32 = jnp.float32
RING = 4
ROWS = 245
PAD = 256
HALF = PAD // 2
CH = 512
COLS = 256
TILE = 16
STRIPS = 35
COPIES = 144
FAR_FIRST = (8, 7, 9, 6, 10, 5, 11, 4, 12, 3, 13, 2, 14, 1, 15)
BAND = 64
PARTS = 4
VMEM_BYTES = 40 * 2**20


def dot(a, b, over):
    return lax.dot_general(a, b, ((over[:1], over[1:]), ((), ())), preferred_element_type=F32)


def picks(step, back=False):
    shape = (STRIPS * TILE, PAD) if back else (PAD, STRIPS * TILE)
    row = lax.broadcasted_iota(jnp.int32, shape, 1 if back else 0)
    col = lax.broadcasted_iota(jnp.int32, shape, 0 if back else 1)
    pixel = col & (TILE - 1)
    wanted = 7 * (col >> 4) + (pixel if step == 1 else pixel >> 1)
    keep = (row == wanted) & (pixel < 7 * step)
    if step == 2:
        keep = keep & ((pixel & 1) == 0)
    return jnp.where(keep, 1.0, 0.0).astype(F32).astype(BF16)


def kernel(
    acts, weight, gain_hbm, shift_hbm, cotan,
    block_out, grad_input, grad_weight, gain_grad, bias_grad,
    raw, strips, w, gain_ref, shift_ref, ct_raw, ct_strips, pick, own, full, ex, mine, gh, hid, cot, acted,
    stat, grad,
    to_sib, from_sib, xb, x_opp, x_left, x_right,
    zb, z_opp, z_left, z_right, share, returned,
    send_sems, recv_sems, local_sems,
):
    section, dp, mp = lax.axis_index("section"), lax.axis_index("dp"), lax.axis_index("mp")
    zh, y = lax.div(dp, RING), lax.rem(dp, RING)
    x, core = lax.div(mp, 2), lax.rem(mp, 2)

    def around(at, by):
        return lax.rem(at + by, RING)

    partner = {"section": section + 1 - 2 * lax.rem(section, 2)}
    sibling = {"mp": 2 * x + 1 - core}
    at_x = [{"mp": 2 * around(x, o) + core} for o in range(RING)]
    at_y = [{"dp": RING * zh + around(y, o)} for o in range(RING)]
    at_z = [{"dp": RING * around(zh, o) + y} for o in range(RING)]
    others = [{"dp": lax.rem(dp + o, RING * RING)} for o in FAR_FIRST]
    peers = [partner, sibling, at_x[1], at_x[3]] + others

    started = []
    ids = iter(range(COPIES))

    def names(n):
        return [next(ids) for _ in range(n)]

    def send(src, dst, k, to):
        copy = pltpu.make_async_remote_copy(
            src_ref=src, dst_ref=dst, send_sem=send_sems.at[k], recv_sem=recv_sems.at[k],
            device_id=to, device_id_type=pl.DeviceIdType.MESH,
        )
        copy.start()
        started.append(copy)

    def arrive(dst, k):
        pltpu.make_async_remote_copy(
            src_ref=dst, dst_ref=dst, send_sem=send_sems.at[k], recv_sem=recv_sems.at[k],
            device_id=sibling, device_id_type=pl.DeviceIdType.MESH,
        ).wait_recv()

    load_acts = pltpu.make_async_copy(acts.at[:, :, 0], raw, local_sems.at[0])
    load_w = pltpu.make_async_copy(weight, w, local_sems.at[1])
    load_ct = pltpu.make_async_copy(cotan, ct_raw, local_sems.at[2])
    load_gain = pltpu.make_async_copy(gain_hbm, gain_ref, local_sems.at[4])
    load_shift = pltpu.make_async_copy(shift_hbm, shift_ref, local_sems.at[5])
    load_acts.start()
    load_ct.start()
    load_w.start()
    load_gain.start()
    load_shift.start()
    barrier = pltpu.get_barrier_semaphore()
    for peer in peers:
        pl.semaphore_signal(barrier, inc=1, device_id=peer, device_id_type=pl.DeviceIdType.MESH)
    strips[:, 14:TILE, :] = jnp.zeros((STRIPS, TILE - 14, CH), BF16)
    ct_strips[...] = jnp.zeros_like(ct_strips)
    choose = picks(2)
    load_acts.wait()
    strips[:, 0:14, :] = raw[...].reshape(STRIPS, 14, CH)
    own[...] = dot(choose, strips[...].reshape(STRIPS * TILE, CH), (1, 0)).astype(BF16)
    pl.semaphore_wait(barrier, len(peers))

    size = PAD // PARTS
    parts = [pl.ds(p * size, size) for p in range(PARTS)]
    k_part, k_left, k_right, k_sib = names(PARTS), names(PARTS), names(PARTS), names(PARTS)
    k_sl, k_sr, k_so, k_opp = names(PARTS), names(PARTS), names(PARTS), names(PARTS)
    for p in range(PARTS):
        send(own.at[parts[p]], full.at[x, core, parts[p]], k_part[p], partner)
    for p in range(PARTS):
        here = full.at[x, core, parts[p]]
        arrive(here, k_part[p])
        send(here, here, k_right[p], at_x[1])
        send(here, here, k_left[p], at_x[3])
        send(here, here, k_sib[p], sibling)
        if p == 0:
            load_ct.wait()
            ct_strips[:, 0:7, :] = ct_raw[...].reshape(STRIPS, 7, COLS)
            cot[...] = dot(picks(1), ct_strips[...].reshape(STRIPS * TILE, COLS), (1, 0))
            pick[...] = picks(1, back=True)
            load_w.wait()
            load_gain.wait()
            load_shift.wait()

    def w_block(xx, cc):
        return w[pl.ds(pl.multiple_of(CH * (2 * xx + cc), CH), CH), :]

    def term(xx, cc):
        return dot(full[xx, cc], w_block(xx, cc), (1, 0))

    k_ex, k_es = [names(3) for _ in range(RING)], names(3)
    my_rows = pl.ds(pl.multiple_of(HALF * core, HALF), HALF)

    def quarter(xx, yy, rows):
        return full.at[xx, lax.div(yy, 2), rows, pl.ds(pl.multiple_of(COLS * lax.rem(yy, 2), COLS), COLS)]

    def ex_rows(yy, cc):
        return pl.ds(pl.multiple_of(PAD * yy + HALF * cc, HALF), HALF)

    def exchange(slot, xx):
        for o in (2, 1, 3):
            yy = around(y, o)
            send(quarter(xx, yy, my_rows), ex.at[xx, ex_rows(y, core)], k_ex[slot][o - 1], at_y[o])

    lx, rx, ox = around(x, 3), around(x, 1), around(x, 2)
    for p in range(PARTS):
        from_left = full.at[lx, core, parts[p]]
        arrive(from_left, k_right[p])
        if p < PARTS // 2:
            send(from_left, from_left, k_opp[p], at_x[1])
        send(from_left, from_left, k_sl[p], sibling)
        from_right = full.at[rx, core, parts[p]]
        arrive(from_right, k_left[p])
        if p >= PARTS // 2:
            send(from_right, from_right, k_opp[p], at_x[3])
        send(from_right, from_right, k_sr[p], sibling)
        if p == 0:
            for q in range(PARTS):
                arrive(full.at[x, 1 - core, parts[q]], k_sib[q])
            exchange(0, x)
    hid[...] = term(x, core)
    hid[...] += term(x, 1 - core)
    hid[...] += term(lx, core)
    hid[...] += term(rx, core)
    for p in range(PARTS):
        arrive(full.at[lx, 1 - core, parts[p]], k_sl[p])
        arrive(full.at[rx, 1 - core, parts[p]], k_sr[p])
    exchange(1, lx)
    exchange(3, rx)
    hid[...] += term(lx, 1 - core)
    hid[...] += term(rx, 1 - core)
    for p in range(PARTS):
        opposite = full.at[ox, core, parts[p]]
        arrive(opposite, k_opp[p])
        send(opposite, opposite, k_so[p], sibling)
    hid[...] += term(ox, core)
    for p in range(PARTS):
        arrive(full.at[ox, 1 - core, parts[p]], k_so[p])
    hid[...] += term(ox, 1 - core)

    def tell(buf, a, b, ks):
        first = lax.broadcasted_iota(jnp.int32, (2, COLS), 0) == 0
        buf[dp] = jnp.where(first, a, b)
        for k, to in zip(ks, others):
            send(buf.at[dp], buf.at[dp], k, to)

    def hear(buf, ks):
        for k, o in zip(ks, FAR_FIRST):
            arrive(buf.at[lax.rem(dp + RING * RING - o, RING * RING)], k)
        return buf[...]

    bands = [pl.ds(b * BAND, BAND) for b in range(PAD // BAND)]
    mean = sum(jnp.sum(hid[band, :], axis=0, keepdims=True) for band in bands) / ROWS
    square = jnp.zeros_like(mean)
    for b, band in enumerate(bands):
        off = hid[band, :] - mean
        if (b + 1) * BAND > ROWS:
            row = lax.broadcasted_iota(jnp.int32, (BAND, COLS), 0)
            off = jnp.where(row < ROWS - b * BAND, off, 0.0)
        square += jnp.sum(off * off, axis=0, keepdims=True)
    k_stat, k_grad = names(15), names(15)
    tell(stat, mean, square, k_stat)
    exchange(2, ox)
    keep = pltpu.make_async_copy(
        full.at[:, lax.div(y, 2), :, pl.ds(pl.multiple_of(COLS * lax.rem(y, 2), COLS), COLS)],
        ex.at[:, pl.ds(pl.multiple_of(PAD * y, PAD), PAD), :],
        local_sems.at[3],
    )
    keep.start()

    heard = hear(stat, k_stat)
    means = heard[:, 0:1, :]
    mean = jnp.sum(means, axis=0) / (RING * RING)
    square = jnp.sum(heard[:, 1:2, :] + ROWS * (means - mean) * (means - mean), axis=0)
    total = float(ROWS * RING * RING)
    inverse = lax.rsqrt(square / total + 1e-05)
    gain, shift = gain_ref[...], shift_ref[...]
    d_bias, d_gain = jnp.zeros_like(mean), jnp.zeros_like(mean)
    for band in bands:
        normed = (hid[band, :] - mean) * inverse
        pre_act = gain * normed + shift
        squash = 0.5 * jnp.tanh(0.5 * pre_act) + 0.5
        acted[band, :] = (pre_act * squash).astype(BF16)
        grad_pre = cot[band, :] * (squash * (1.0 + pre_act * (1.0 - squash)))
        cot[band, :] = grad_pre
        d_bias += jnp.sum(grad_pre, axis=0, keepdims=True)
        d_gain += jnp.sum(grad_pre * normed, axis=0, keepdims=True)
    tell(grad, d_bias, d_gain, k_grad)

    for o in (1, 3, 2):
        rows = ex_rows(around(y, RING - o), core)
        for slot, xx in enumerate((x, lx, ox, rx)):
            arrive(ex.at[xx, rows], k_ex[slot][o - 1])
        send(ex.at[:, rows], ex.at[:, rows], k_es[o - 1], sibling)

    sums = jnp.sum(hear(grad, k_grad), axis=0)
    d_bias, d_gain = sums[0:1, :], sums[1:2, :]
    scale = gain * inverse
    less, tilt = d_bias / total, inverse * (d_gain / total)
    for band in bands:
        part = scale * (cot[band, :] - less - (hid[band, :] - mean) * tilt)
        mine[band, :] = part.astype(BF16)

    k_up, k_down, k_far = names(4), names(4), names(4)
    order = (2, 1, 3, 0)

    def gh_rows(j, yy, h):
        return gh.at[j, pl.ds(pl.multiple_of(PAD * yy + HALF * h, HALF), HALF), :]

    for j in range(2):
        gh[j, pl.ds(pl.multiple_of(PAD * y, PAD), PAD), :] = mine[:, HALF * j : HALF * (j + 1)]
        for h in range(2):
            send(gh_rows(j, y, h), gh_rows(j, y, h), k_up[2 * j + h], at_y[1])
            send(gh_rows(j, y, 1 - h), gh_rows(j, y, 1 - h), k_down[2 * j + 1 - h], at_y[3])

    k_cs = names(4)
    for o in order:
        to_sib[o] = dot(mine[...], w_block(around(x, o), 1 - core), (1, 1)).astype(BF16)
        send(to_sib.at[o], from_sib.at[o], k_cs[o], sibling)

    ly, ry, oy = around(y, 3), around(y, 1), around(y, 2)
    for j in range(2):
        arrive(gh_rows(j, ly, 0), k_up[2 * j])
        send(gh_rows(j, ly, 0), gh_rows(j, ly, 0), k_far[2 * j], at_y[1])
        arrive(gh_rows(j, ry, 1), k_down[2 * j + 1])
        send(gh_rows(j, ry, 1), gh_rows(j, ry, 1), k_far[2 * j + 1], at_y[3])

    def ring_start(block, opp, left, right, to, ks):
        mid = block.shape[1] // 2
        lo, hi = pl.ds(0, mid), pl.ds(mid, mid)
        send(block.at[2, lo], opp.at[lo], ks[0], to[1])
        send(block.at[2, hi], opp.at[hi], ks[1], to[3])
        send(block.at[1, hi], left.at[hi], ks[2], to[1])
        send(block.at[3, lo], right.at[lo], ks[3], to[3])

    def ring_middle(block, opp, left, right, to, ks):
        mid = block.shape[1] // 2
        lo, hi = pl.ds(0, mid), pl.ds(mid, mid)
        arrive(opp.at[lo], ks[0])
        block[1, lo] = (block[1, lo].astype(F32) + opp[lo].astype(F32)).astype(BF16)
        send(block.at[1, lo], left.at[lo], ks[4], to[1])
        arrive(opp.at[hi], ks[1])
        block[3, hi] = (block[3, hi].astype(F32) + opp[hi].astype(F32)).astype(BF16)
        send(block.at[3, hi], right.at[hi], ks[5], to[3])

    def ring_end(block, left, right, ks):
        mid = block.shape[1] // 2
        lo, hi = pl.ds(0, mid), pl.ds(mid, mid)
        arrive(left.at[hi], ks[2])
        arrive(right.at[lo], ks[3])
        arrive(left.at[lo], ks[4])
        arrive(right.at[hi], ks[5])
        return block[0].astype(F32) + left[...].astype(F32) + right[...].astype(F32)

    k_x, k_z, k_back = names(6), [names(6), names(6)], names(1)
    for o in order:
        part = dot(mine[...], w_block(around(x, o), core), (1, 1))
        arrive(from_sib.at[o], k_cs[o])
        xb[o] = (part + from_sib[o].astype(F32)).astype(BF16)
    ring_x = (xb, x_opp, x_left, x_right)
    ring_start(*ring_x, at_x, k_x)

    keep.wait()
    for o in (1, 3, 2):
        rows = ex_rows(around(y, RING - o), 1 - core)
        arrive(ex.at[:, rows], k_es[o - 1])
    ring_z = [[ref.at[j] for ref in (zb, z_opp, z_left, z_right)] for j in range(2)]
    for j in range(2):
        arrive(gh_rows(j, ly, 1), k_up[2 * j + 1])
        arrive(gh_rows(j, ry, 0), k_down[2 * j])
        arrive(gh_rows(j, oy, 0), k_far[2 * j])
        arrive(gh_rows(j, oy, 1), k_far[2 * j + 1])
        across = gh[j].T
        for o in order:
            zb[j, o] = dot(across, ex[around(zh, o)], (1, 0)).astype(BF16)
        ring_start(*ring_z[j], at_z, k_z[j])

    spaced = dot(pick[...], acted[...], (1, 0)).reshape(STRIPS, TILE, COLS)
    block_out[...] = spaced[:, 0:7, :].astype(BF16)
    bias_grad[...] = d_bias
    gain_grad[...] = d_gain

    ring_middle(*ring_x, at_x, k_x)
    ring_middle(*ring_z[0], at_z, k_z[0])
    share[...] = ring_end(xb, x_left, x_right, k_x).astype(BF16)
    send(share, returned, k_back[0], partner)
    ring_middle(*ring_z[1], at_z, k_z[1])
    for j in range(2):
        block, _, left, right = ring_z[j]
        grad_weight[:, HALF * j : HALF * (j + 1)] = ring_end(block, left, right, k_z[j]).T.astype(BF16)

    arrive(returned, k_back[0])
    spaced = dot(pick[...], returned[...], (1, 0)).reshape(STRIPS, TILE, CH)
    grad_input[...] = spaced[:, 0:7, :].astype(BF16)
    for copy in started:
        copy.wait_send()


def on_device(activations, conv_weight, norm_gain, norm_bias, cotangent):
    images = activations.shape[1]
    acts = activations.reshape(images, 7, 2, 14, CH)
    cotan = cotangent.reshape(images, 7, 7, COLS)
    hbm = pl.BlockSpec(memory_space=pltpu.HBM)
    results = (
        jax.ShapeDtypeStruct((STRIPS, 7, COLS), BF16),
        jax.ShapeDtypeStruct((STRIPS, 7, CH), BF16),
        jax.ShapeDtypeStruct((COLS, COLS), BF16),
        jax.ShapeDtypeStruct((1, COLS), F32),
        jax.ShapeDtypeStruct((1, COLS), F32),
    )
    block_out, grad_input, grad_weight, gain_grad, bias_grad = pl.pallas_call(
        kernel,
        out_shape=results,
        in_specs=[hbm] * 5,
        out_specs=[pl.BlockSpec(memory_space=pltpu.VMEM)] * 5,
        scratch_shapes=[
            pltpu.VMEM((images, 7, 14, CH), BF16),
            pltpu.VMEM((STRIPS, TILE, CH), BF16),
            pltpu.VMEM((RING * 2 * CH, COLS), BF16),
            pltpu.VMEM((1, COLS), F32),
            pltpu.VMEM((1, COLS), F32),
            pltpu.VMEM((images, 7, 7, COLS), BF16),
            pltpu.VMEM((STRIPS, TILE, COLS), BF16),
            pltpu.VMEM((STRIPS * TILE, PAD), BF16),
            pltpu.VMEM((PAD, CH), BF16),
            pltpu.VMEM((RING, 2, PAD, CH), BF16),
            pltpu.VMEM((RING, RING * PAD, COLS), BF16),
            pltpu.VMEM((PAD, COLS), BF16),
            pltpu.VMEM((2, RING * PAD, HALF), BF16),
            pltpu.VMEM((PAD, COLS), F32),
            pltpu.VMEM((PAD, COLS), F32),
            pltpu.VMEM((PAD, COLS), BF16),
            pltpu.VMEM((RING * RING, 2, COLS), F32),
            pltpu.VMEM((RING * RING, 2, COLS), F32),
            pltpu.VMEM((RING, PAD, CH), BF16),
            pltpu.VMEM((RING, PAD, CH), BF16),
            pltpu.VMEM((RING, PAD, CH), BF16),
            pltpu.VMEM((PAD, CH), BF16),
            pltpu.VMEM((PAD, CH), BF16),
            pltpu.VMEM((PAD, CH), BF16),
            pltpu.VMEM((2, RING, HALF, COLS), BF16),
            pltpu.VMEM((2, HALF, COLS), BF16),
            pltpu.VMEM((2, HALF, COLS), BF16),
            pltpu.VMEM((2, HALF, COLS), BF16),
            pltpu.VMEM((PAD, CH), BF16),
            pltpu.VMEM((PAD, CH), BF16),
            pltpu.SemaphoreType.DMA((COPIES,)),
            pltpu.SemaphoreType.DMA((COPIES,)),
            pltpu.SemaphoreType.DMA((6,)),
        ],
        compiler_params=pltpu.CompilerParams(
            collective_id=0, has_side_effects=True, vmem_limit_bytes=VMEM_BYTES
        ),
        name="bottleneck",
    )(*(pltpu.with_memory_space_constraint(a, pltpu.HBM) for a in (acts, conv_weight[0], norm_gain, norm_bias, cotan)))
    return (
        block_out.reshape(1, images, 7, 7, COLS),
        grad_input.reshape(1, images, 7, 7, CH),
        grad_weight[None],
        gain_grad,
        bias_grad,
    )


def solution(mesh):
    placed = (
        P("section", "dp", None, None, "mp"),
        P("section", None, "mp"),
        P("section", "mp"),
        P("section", "mp"),
        P("section", "dp", None, None, "mp"),
    )
    return jax.shard_map(
        on_device,
        mesh=mesh,
        in_specs=placed,
        out_specs=(
            P("section", "dp", None, None, "mp"),
            P("section", "dp", None, None, "mp"),
            P("section", "dp", "mp"),
            P("section", "mp"),
            P("section", "mp"),
        ),
        check_vma=False,
    )
```

time: 449 us -> 87.7 us (0.20)
  waiting for transfers between devices: 244 us -> 0 us
  blocking collectives: 150 us -> 0 us
  Pallas kernels: 0 us -> 83.7 us
  local copies, waits for them, and re-layouts: 24.5 us -> 3.15 us
  between operations: 13.8 us -> 0.64 us
  matrix products: 7.98 us -> 0 us
  starting transfers between devices: 7.08 us -> 0 us
    reduce_scatter x2 -> x0, waiting for transfers between devices: 157 us -> none  [the longest x1 130 us: on_device(): lax.psum_scatter(lax.dot_general(pixel_rows, grad_hidden, (((0,), (0,)),...]
    psum x3 -> x0, blocking collectives: 150 us -> none  [the longest x1 54.9 us: on_device(): average = lax.psum(jnp.sum(hidden, axis=0), 'dp') / total_rows]
    pallas_call x0 -> x1, Pallas kernels: none -> 83.7 us  [on_device(): pl.pallas_call(kernel, out_shape=results, in_specs=[hbm] * 5, out_specs=[...]
    ppermute x2 -> x0, waiting for transfers between devices: 49.8 us -> none  [from_partner(): return lax.ppermute(value, axis, pairs)]
    all_gather x1 -> x0, waiting for transfers between devices: 36.6 us -> none  [on_device(): complete = lax.all_gather(sampled, 'mp', axis=3, tiled=True)]
    slice x1 -> x0, local copies, waits for them, and re-layouts: 16.8 us -> none  [on_device(): sampled = activations[0][:, ::2, ::2, :]]
    dot_general x3 -> x0, matrix products: 7.98 us -> none  [the longest x1 3.65 us: on_device(): lax.dot_general(pixel_rows, grad_hidden, (((0,), (0,)), ((), ())), prefer...]
    ppermute x2 -> x0, starting transfers between devices: 6.96 us -> none  [from_partner(): return lax.ppermute(value, axis, pairs)]
  transfers between devices with their start and end apart: 5 -> 0, of which waited for: 4 -> 0; matrix products, arithmetic and copies ran while one was open for 2% -> 0% of each run, Pallas kernels for 0% -> 0%
where the time goes in v2:
time: 87.7 us; the launch traced here: 87.5 us
  Pallas kernels  83.7 us (95%)
  local copies, waits for them, and re-layouts  3.15 us (4%)
    pallas_call x1, Pallas kernels, on_device(): pl.pallas_call(kernel, out_shape=results, in_specs=[hbm] * 5, out_specs=[...  83.7 us
    unnamed x5, local copies, waits for them, and re-layouts  3.15 us

profile of v2, /device:TPU:6, one launch (start us, length us, event | category | flops | bytes accessed | tf_op | source)
XLA Modules:
  0.0 87.5 jit_solution(2340247912764530048)
XLA Ops:
  0.6 83.7 %bottleneck.1 = (bf16[35,7,256]{2,1,0:T(8,128)(2,1)S(1)}, bf16[35,7,512]{2,1,0:T(8,128)(2,1)S(1)}, bf16[256,256]{1,0:T(8,128)(2,1)S(1)}, f32[1,256]{1,0:T(1,128)S(1)}, f32[1,256]{1,0:T(1,128)S(1)}) custom-call(bf16[5,7,2,14,512]{4,3,2,1,0:T(8,128)(2,1)} %bitcast.10, bf16[4096,256]{1,0:T(8,128)(2,1)} %bitcast.9, f32[1,256]{1,0:T(1,128)} %gain_hbm.1, ...), custom_call_target="tpu_custom_call" | custom-call | tf_op jit(solution)/shard_map/bottleneck/pallas_call | solution.py:355
  84.4 0.7 copy.15
  85.0 0.7 copy.16
  85.7 0.7 copy.17
  86.4 0.6 copy.18
  87.0 0.6 copy.19

commit v3 on v2

--- a/solution.py
+++ b/solution.py
@@ -17,7 +17,7 @@
 COLS = 256
 TILE = 16
 STRIPS = 35
-COPIES = 144
+COPIES = 160
 FAR_FIRST = (8, 7, 9, 6, 10, 5, 11, 4, 12, 3, 13, 2, 14, 1, 15)
 BAND = 64
 PARTS = 4
@@ -28,10 +28,11 @@
     return lax.dot_general(a, b, ((over[:1], over[1:]), ((), ())), preferred_element_type=F32)
 
 
-def picks(step, back=False):
-    shape = (STRIPS * TILE, PAD) if back else (PAD, STRIPS * TILE)
-    row = lax.broadcasted_iota(jnp.int32, shape, 1 if back else 0)
-    col = lax.broadcasted_iota(jnp.int32, shape, 0 if back else 1)
+def picks(step, back=False, rows=(0, PAD), strips=(0, STRIPS)):
+    shape = (rows[1] - rows[0], (strips[1] - strips[0]) * TILE)
+    shape = shape[::-1] if back else shape
+    row = rows[0] + lax.broadcasted_iota(jnp.int32, shape, 1 if back else 0)
+    col = strips[0] * TILE + lax.broadcasted_iota(jnp.int32, shape, 0 if back else 1)
     pixel = col & (TILE - 1)
     wanted = 7 * (col >> 4) + (pixel if step == 1 else pixel >> 1)
     keep = (row == wanted) & (pixel < 7 * step)
@@ -42,12 +43,12 @@
 
 def kernel(
     acts, weight, gain_hbm, shift_hbm, cotan,
-    block_out, grad_input, grad_weight, gain_grad, bias_grad,
-    raw, strips, w, gain_ref, shift_ref, ct_raw, ct_strips, pick, own, full, ex, mine, gh, hid, cot, acted,
+    block_out, grad_input, grad_weight, grads,
+    raw, strips, w, gain_ref, shift_ref, ct_raw, ct_strips, pick, own, full, ex, own_rows, mine, gh, hid, cot, acted,
     stat, grad,
     to_sib, from_sib, xb, x_opp, x_left, x_right,
     zb, z_opp, z_left, z_right, share, returned,
-    send_sems, recv_sems, local_sems,
+    send_sems, recv_sems, local_sems, met_sem,
 ):
     section, dp, mp = lax.axis_index("section"), lax.axis_index("dp"), lax.axis_index("mp")
     zh, y = lax.div(dp, RING), lax.rem(dp, RING)
@@ -62,7 +63,8 @@
     at_y = [{"dp": RING * zh + around(y, o)} for o in range(RING)]
     at_z = [{"dp": RING * around(zh, o) + y} for o in range(RING)]
     others = [{"dp": lax.rem(dp + o, RING * RING)} for o in FAR_FIRST]
-    peers = [partner, sibling, at_x[1], at_x[3]] + others
+    near = [partner, at_x[1], at_x[3]] + at_y[1:]
+    far = [{"dp": RING * around(zh, i) + around(y, j)} for i in (2, 1, 3) for j in range(RING)]
 
     started = []
     ids = iter(range(COPIES))
@@ -84,33 +86,65 @@
             device_id=sibling, device_id_type=pl.DeviceIdType.MESH,
         ).wait_recv()
 
-    load_acts = pltpu.make_async_copy(acts.at[:, :, 0], raw, local_sems.at[0])
+    early = 2
+    load_first = pltpu.make_async_copy(acts.at[0:early, :, 0], raw.at[0:early], local_sems.at[0])
+    load_rest = pltpu.make_async_copy(acts.at[early:, :, 0], raw.at[early:], local_sems.at[6])
     load_w = pltpu.make_async_copy(weight, w, local_sems.at[1])
     load_ct = pltpu.make_async_copy(cotan, ct_raw, local_sems.at[2])
     load_gain = pltpu.make_async_copy(gain_hbm, gain_ref, local_sems.at[4])
     load_shift = pltpu.make_async_copy(shift_hbm, shift_ref, local_sems.at[5])
-    load_acts.start()
+    load_first.start()
+    load_rest.start()
     load_ct.start()
     load_w.start()
     load_gain.start()
     load_shift.start()
     barrier = pltpu.get_barrier_semaphore()
-    for peer in peers:
-        pl.semaphore_signal(barrier, inc=1, device_id=peer, device_id_type=pl.DeviceIdType.MESH)
+
+    def signal(sem, to):
+        pl.semaphore_signal(sem, inc=1, device_id=to, device_id_type=pl.DeviceIdType.MESH)
+
+    @pl.when(core == 1)
+    def _():
+        signal(barrier, sibling)
+
+    for to in near:
+        signal(barrier, {"mp": 2 * x, **to, **({"mp": to["mp"] - core} if "mp" in to else {})})
+    for to in far:
+        signal(barrier, {"mp": 2 * x + 1, **to})
     strips[:, 14:TILE, :] = jnp.zeros((STRIPS, TILE - 14, CH), BF16)
-    ct_strips[...] = jnp.zeros_like(ct_strips)
-    choose = picks(2)
-    load_acts.wait()
-    strips[:, 0:14, :] = raw[...].reshape(STRIPS, 14, CH)
-    own[...] = dot(choose, strips[...].reshape(STRIPS * TILE, CH), (1, 0)).astype(BF16)
-    pl.semaphore_wait(barrier, len(peers))
-
     size = PAD // PARTS
     parts = [pl.ds(p * size, size) for p in range(PARTS)]
+
+    def sample(p):
+        first, last = p * size // 7, min(((p + 1) * size - 1) // 7 + 1, STRIPS)
+        choose = picks(2, rows=(p * size, (p + 1) * size), strips=(first, last))
+        pixels = strips[first:last].reshape((last - first) * TILE, CH)
+        own[parts[p], :] = dot(choose, pixels, (1, 0)).astype(BF16)
+
+    load_first.wait()
+    strips[0 : 7 * early, 0:14, :] = raw[0:early].reshape(7 * early, 14, CH)
+    sample(0)
+    @pl.when(core == 0)
+    def _():
+        pl.semaphore_wait(barrier, 2 * len(near) + 1)
+        signal(met_sem, sibling)
+
+    @pl.when(core == 1)
+    def _():
+        pl.semaphore_wait(met_sem, 1)
+
+
     k_part, k_left, k_right, k_sib = names(PARTS), names(PARTS), names(PARTS), names(PARTS)
     k_sl, k_sr, k_so, k_opp = names(PARTS), names(PARTS), names(PARTS), names(PARTS)
     for p in range(PARTS):
+        if p == 1:
+            load_rest.wait()
+            strips[7 * early :, 0:14, :] = raw[early:].reshape(STRIPS - 7 * early, 14, CH)
+        if p > 0:
+            sample(p)
         send(own.at[parts[p]], full.at[x, core, parts[p]], k_part[p], partner)
+    ct_strips[...] = jnp.zeros_like(ct_strips)
     for p in range(PARTS):
         here = full.at[x, core, parts[p]]
         arrive(here, k_part[p])
@@ -132,19 +166,44 @@
     def term(xx, cc):
         return dot(full[xx, cc], w_block(xx, cc), (1, 0))
 
-    k_ex, k_es = [names(3) for _ in range(RING)], names(3)
-    my_rows = pl.ds(pl.multiple_of(HALF * core, HALF), HALF)
-
-    def quarter(xx, yy, rows):
-        return full.at[xx, lax.div(yy, 2), rows, pl.ds(pl.multiple_of(COLS * lax.rem(yy, 2), COLS), COLS)]
-
-    def ex_rows(yy, cc):
-        return pl.ds(pl.multiple_of(PAD * yy + HALF * cc, HALF), HALF)
-
-    def exchange(slot, xx):
+    k_ex, k_xl, k_xr, k_xo, k_es = names(RING), names(2), names(2), names(2), names(RING)
+
+    def exchange():
         for o in (2, 1, 3):
             yy = around(y, o)
-            send(quarter(xx, yy, my_rows), ex.at[xx, ex_rows(y, core)], k_ex[slot][o - 1], at_y[o])
+            at = pl.multiple_of(COLS * lax.rem(yy, 2), COLS)
+            rows = pl.ds(pl.multiple_of(HALF * core, HALF), HALF)
+            send(
+                full.at[x, lax.div(yy, 2), rows, pl.ds(at, COLS)],
+                ex.at[x, RING - o, core], k_ex[o], at_y[o],
+            )
+
+    def others_of(xx, cc, h=None):
+        rows = pl.ds(0, HALF) if h is None else pl.ds(h * BAND, BAND)
+        return ex.at[xx, pl.ds(1, RING - 1), cc, rows]
+
+    def along_x():
+        for o in range(1, RING):
+            arrive(ex.at[x, RING - o, core], k_ex[o])
+        for h in range(2):
+            send(others_of(x, core, h), others_of(x, core, h), k_xl[h], at_x[1])
+            send(others_of(x, core, 1 - h), others_of(x, core, 1 - h), k_xr[1 - h], at_x[3])
+        send(others_of(x, core), others_of(x, core), k_es[0], sibling)
+
+    def farther_x():
+        arrive(others_of(lx, core, 0), k_xl[0])
+        send(others_of(lx, core, 0), others_of(lx, core, 0), k_xo[0], at_x[1])
+        arrive(others_of(rx, core, 1), k_xr[1])
+        send(others_of(rx, core, 1), others_of(rx, core, 1), k_xo[1], at_x[3])
+        arrive(others_of(lx, core, 1), k_xl[1])
+        send(others_of(lx, core), others_of(lx, core), k_es[1], sibling)
+        arrive(others_of(rx, core, 0), k_xr[0])
+        send(others_of(rx, core), others_of(rx, core), k_es[2], sibling)
+
+    def last_x():
+        arrive(others_of(ox, core, 0), k_xo[0])
+        arrive(others_of(ox, core, 1), k_xo[1])
+        send(others_of(ox, core), others_of(ox, core), k_es[3], sibling)
 
     lx, rx, ox = around(x, 3), around(x, 1), around(x, 2)
     for p in range(PARTS):
@@ -161,7 +220,7 @@
         if p == 0:
             for q in range(PARTS):
                 arrive(full.at[x, 1 - core, parts[q]], k_sib[q])
-            exchange(0, x)
+            exchange()
     hid[...] = term(x, core)
     hid[...] += term(x, 1 - core)
     hid[...] += term(lx, core)
@@ -169,8 +228,6 @@
     for p in range(PARTS):
         arrive(full.at[lx, 1 - core, parts[p]], k_sl[p])
         arrive(full.at[rx, 1 - core, parts[p]], k_sr[p])
-    exchange(1, lx)
-    exchange(3, rx)
     hid[...] += term(lx, 1 - core)
     hid[...] += term(rx, 1 - core)
     for p in range(PARTS):
@@ -203,12 +260,20 @@
             off = jnp.where(row < ROWS - b * BAND, off, 0.0)
         square += jnp.sum(off * off, axis=0, keepdims=True)
     k_stat, k_grad = names(15), names(15)
+    @pl.when(core == 1)
+    def _():
+        pl.semaphore_wait(barrier, 2 * len(far))
+        signal(met_sem, sibling)
+
+    @pl.when(core == 0)
+    def _():
+        pl.semaphore_wait(met_sem, 1)
+
     tell(stat, mean, square, k_stat)
-    exchange(2, ox)
+    along_x()
     keep = pltpu.make_async_copy(
         full.at[:, lax.div(y, 2), :, pl.ds(pl.multiple_of(COLS * lax.rem(y, 2), COLS), COLS)],
-        ex.at[:, pl.ds(pl.multiple_of(PAD * y, PAD), PAD), :],
-        local_sems.at[3],
+        own_rows, local_sems.at[3],
     )
     keep.start()
 
@@ -231,12 +296,7 @@
         d_gain += jnp.sum(grad_pre * normed, axis=0, keepdims=True)
     tell(grad, d_bias, d_gain, k_grad)
 
-    for o in (1, 3, 2):
-        rows = ex_rows(around(y, RING - o), core)
-        for slot, xx in enumerate((x, lx, ox, rx)):
-            arrive(ex.at[xx, rows], k_ex[slot][o - 1])
-        send(ex.at[:, rows], ex.at[:, rows], k_es[o - 1], sibling)
-
+    farther_x()
     sums = jnp.sum(hear(grad, k_grad), axis=0)
     d_bias, d_gain = sums[0:1, :], sums[1:2, :]
     scale = gain * inverse
@@ -245,29 +305,33 @@
         part = scale * (cot[band, :] - less - (hid[band, :] - mean) * tilt)
         mine[band, :] = part.astype(BF16)
 
+    halves = [pl.ds(0, HALF), pl.ds(HALF, HALF)]
+
     k_up, k_down, k_far = names(4), names(4), names(4)
     order = (2, 1, 3, 0)
 
-    def gh_rows(j, yy, h):
-        return gh.at[j, pl.ds(pl.multiple_of(PAD * yy + HALF * h, HALF), HALF), :]
+    def gh_rows(j, r, h):
+        return gh.at[j, pl.ds(PAD * r + HALF * h, HALF), :]
 
     for j in range(2):
-        gh[j, pl.ds(pl.multiple_of(PAD * y, PAD), PAD), :] = mine[:, HALF * j : HALF * (j + 1)]
+        gh[j, 0:PAD, :] = mine[:, HALF * j : HALF * (j + 1)]
         for h in range(2):
-            send(gh_rows(j, y, h), gh_rows(j, y, h), k_up[2 * j + h], at_y[1])
-            send(gh_rows(j, y, 1 - h), gh_rows(j, y, 1 - h), k_down[2 * j + 1 - h], at_y[3])
-
-    k_cs = names(4)
-    for o in order:
-        to_sib[o] = dot(mine[...], w_block(around(x, o), 1 - core), (1, 1)).astype(BF16)
-        send(to_sib.at[o], from_sib.at[o], k_cs[o], sibling)
-
-    ly, ry, oy = around(y, 3), around(y, 1), around(y, 2)
+            send(gh_rows(j, 0, h), gh_rows(j, 3, h), k_up[2 * j + h], at_y[1])
+            send(gh_rows(j, 0, 1 - h), gh_rows(j, 1, 1 - h), k_down[2 * j + 1 - h], at_y[3])
+
+    k_cs = [names(4), names(4)]
+    for q in range(2):
+        for o in order:
+            part = dot(mine[halves[q], :], w_block(around(x, o), 1 - core), (1, 1))
+            to_sib[q, o] = part.astype(BF16)
+            send(to_sib.at[q, o], from_sib.at[q, o], k_cs[q][o], sibling)
+
+    last_x()
     for j in range(2):
-        arrive(gh_rows(j, ly, 0), k_up[2 * j])
-        send(gh_rows(j, ly, 0), gh_rows(j, ly, 0), k_far[2 * j], at_y[1])
-        arrive(gh_rows(j, ry, 1), k_down[2 * j + 1])
-        send(gh_rows(j, ry, 1), gh_rows(j, ry, 1), k_far[2 * j + 1], at_y[3])
+        arrive(gh_rows(j, 3, 0), k_up[2 * j])
+        send(gh_rows(j, 3, 0), gh_rows(j, 2, 0), k_far[2 * j], at_y[1])
+        arrive(gh_rows(j, 1, 1), k_down[2 * j + 1])
+        send(gh_rows(j, 1, 1), gh_rows(j, 2, 1), k_far[2 * j + 1], at_y[3])
 
     def ring_start(block, opp, left, right, to, ks):
         mid = block.shape[1] // 2
@@ -296,44 +360,59 @@
         arrive(right.at[hi], ks[5])
         return block[0].astype(F32) + left[...].astype(F32) + right[...].astype(F32)
 
-    k_x, k_z, k_back = names(6), [names(6), names(6)], names(1)
-    for o in order:
-        part = dot(mine[...], w_block(around(x, o), core), (1, 1))
-        arrive(from_sib.at[o], k_cs[o])
-        xb[o] = (part + from_sib[o].astype(F32)).astype(BF16)
-    ring_x = (xb, x_opp, x_left, x_right)
-    ring_start(*ring_x, at_x, k_x)
-
-    keep.wait()
-    for o in (1, 3, 2):
-        rows = ex_rows(around(y, RING - o), 1 - core)
-        arrive(ex.at[:, rows], k_es[o - 1])
+    k_x, k_z, k_back = [names(6), names(6)], [names(6), names(6)], names(2)
+    ring_x = [[ref.at[q] for ref in (xb, x_opp, x_left, x_right)] for q in range(2)]
     ring_z = [[ref.at[j] for ref in (zb, z_opp, z_left, z_right)] for j in range(2)]
-    for j in range(2):
-        arrive(gh_rows(j, ly, 1), k_up[2 * j + 1])
-        arrive(gh_rows(j, ry, 0), k_down[2 * j])
-        arrive(gh_rows(j, oy, 0), k_far[2 * j])
-        arrive(gh_rows(j, oy, 1), k_far[2 * j + 1])
+
+    def start_x(q):
+        for o in order:
+            part = dot(mine[halves[q], :], w_block(around(x, o), core), (1, 1))
+            arrive(from_sib.at[q, o], k_cs[q][o])
+            xb[q, o] = (part + from_sib[q, o].astype(F32)).astype(BF16)
+        ring_start(*ring_x[q], at_x, k_x[q])
+
+    def start_z(j):
+        arrive(gh_rows(j, 3, 1), k_up[2 * j + 1])
+        arrive(gh_rows(j, 1, 0), k_down[2 * j])
+        arrive(gh_rows(j, 2, 0), k_far[2 * j])
+        arrive(gh_rows(j, 2, 1), k_far[2 * j + 1])
         across = gh[j].T
         for o in order:
-            zb[j, o] = dot(across, ex[around(zh, o)], (1, 0)).astype(BF16)
+            slot = around(zh, o)
+            rest = ex[slot, 1:RING].reshape((RING - 1) * PAD, COLS)
+            block = dot(across[:, 0:PAD], own_rows[slot], (1, 0))
+            zb[j, o] = (block + dot(across[:, PAD:], rest, (1, 0))).astype(BF16)
         ring_start(*ring_z[j], at_z, k_z[j])
+
+    def give_back(q):
+        block, _, left, right = ring_x[q]
+        share[halves[q], :] = ring_end(block, left, right, k_x[q]).astype(BF16)
+        send(share.at[halves[q]], returned.at[halves[q]], k_back[q], partner)
+
+    start_x(0)
+    keep.wait()
+    for i, xx in enumerate((x, lx, rx, ox)):
+        arrive(others_of(xx, 1 - core), k_es[i])
+    start_z(0)
+    start_x(1)
+    start_z(1)
 
     spaced = dot(pick[...], acted[...], (1, 0)).reshape(STRIPS, TILE, COLS)
     block_out[...] = spaced[:, 0:7, :].astype(BF16)
-    bias_grad[...] = d_bias
-    gain_grad[...] = d_gain
-
-    ring_middle(*ring_x, at_x, k_x)
+    grads[...] = sums
+
+    ring_middle(*ring_x[0], at_x, k_x[0])
     ring_middle(*ring_z[0], at_z, k_z[0])
-    share[...] = ring_end(xb, x_left, x_right, k_x).astype(BF16)
-    send(share, returned, k_back[0], partner)
+    ring_middle(*ring_x[1], at_x, k_x[1])
+    give_back(0)
     ring_middle(*ring_z[1], at_z, k_z[1])
+    give_back(1)
     for j in range(2):
         block, _, left, right = ring_z[j]
         grad_weight[:, HALF * j : HALF * (j + 1)] = ring_end(block, left, right, k_z[j]).T.astype(BF16)
 
-    arrive(returned, k_back[0])
+    for q in range(2):
+        arrive(returned.at[halves[q]], k_back[q])
     spaced = dot(pick[...], returned[...], (1, 0)).reshape(STRIPS, TILE, CH)
     grad_input[...] = spaced[:, 0:7, :].astype(BF16)
     for copy in started:
@@ -349,14 +428,13 @@
         jax.ShapeDtypeStruct((STRIPS, 7, COLS), BF16),
         jax.ShapeDtypeStruct((STRIPS, 7, CH), BF16),
         jax.ShapeDtypeStruct((COLS, COLS), BF16),
-        jax.ShapeDtypeStruct((1, COLS), F32),
-        jax.ShapeDtypeStruct((1, COLS), F32),
+        jax.ShapeDtypeStruct((2, COLS), F32),
     )
-    block_out, grad_input, grad_weight, gain_grad, bias_grad = pl.pallas_call(
+    block_out, grad_input, grad_weight, grads = pl.pallas_call(
         kernel,
         out_shape=results,
         in_specs=[hbm] * 5,
-        out_specs=[pl.BlockSpec(memory_space=pltpu.VMEM)] * 5,
+        out_specs=[pl.BlockSpec(memory_space=pltpu.VMEM)] * 4,
         scratch_shapes=[
             pltpu.VMEM((images, 7, 14, CH), BF16),
             pltpu.VMEM((STRIPS, TILE, CH), BF16),
@@ -368,7 +446,8 @@
             pltpu.VMEM((STRIPS * TILE, PAD), BF16),
             pltpu.VMEM((PAD, CH), BF16),
             pltpu.VMEM((RING, 2, PAD, CH), BF16),
-            pltpu.VMEM((RING, RING * PAD, COLS), BF16),
+            pltpu.VMEM((RING, RING, 2, HALF, COLS), BF16),
+            pltpu.VMEM((RING, PAD, COLS), BF16),
             pltpu.VMEM((PAD, COLS), BF16),
             pltpu.VMEM((2, RING * PAD, HALF), BF16),
             pltpu.VMEM((PAD, COLS), F32),
@@ -376,12 +455,12 @@
             pltpu.VMEM((PAD, COLS), BF16),
             pltpu.VMEM((RING * RING, 2, COLS), F32),
             pltpu.VMEM((RING * RING, 2, COLS), F32),
-            pltpu.VMEM((RING, PAD, CH), BF16),
-            pltpu.VMEM((RING, PAD, CH), BF16),
-            pltpu.VMEM((RING, PAD, CH), BF16),
-            pltpu.VMEM((PAD, CH), BF16),
-            pltpu.VMEM((PAD, CH), BF16),
-            pltpu.VMEM((PAD, CH), BF16),
+            pltpu.VMEM((2, RING, HALF, CH), BF16),
+            pltpu.VMEM((2, RING, HALF, CH), BF16),
+            pltpu.VMEM((2, RING, HALF, CH), BF16),
+            pltpu.VMEM((2, HALF, CH), BF16),
+            pltpu.VMEM((2, HALF, CH), BF16),
+            pltpu.VMEM((2, HALF, CH), BF16),
             pltpu.VMEM((2, RING, HALF, COLS), BF16),
             pltpu.VMEM((2, HALF, COLS), BF16),
             pltpu.VMEM((2, HALF, COLS), BF16),
@@ -390,7 +469,8 @@
             pltpu.VMEM((PAD, CH), BF16),
             pltpu.SemaphoreType.DMA((COPIES,)),
             pltpu.SemaphoreType.DMA((COPIES,)),
-            pltpu.SemaphoreType.DMA((6,)),
+            pltpu.SemaphoreType.DMA((7,)),
+            pltpu.SemaphoreType.REGULAR,
         ],
         compiler_params=pltpu.CompilerParams(
             collective_id=0, has_side_effects=True, vmem_limit_bytes=VMEM_BYTES
@@ -401,8 +481,8 @@
         block_out.reshape(1, images, 7, 7, COLS),
         grad_input.reshape(1, images, 7, 7, CH),
         grad_weight[None],
-        gain_grad,
-        bias_grad,
+        grads[1:2],
+        grads[0:1],
     )
 
 

time: 87.7 us -> 82.8 us (0.944)
  Pallas kernels: 83.7 us -> 79.4 us
    pallas_call x1, Pallas kernels: 83.7 us -> 79.4 us  [on_device(): pl.pallas_call(kernel, out_shape=results, in_specs=[hbm] * 5, out_specs=[...]
    unnamed x5 -> x3, local copies, waits for them, and re-layouts: 3.15 us -> 2.02 us
where the time goes in v3:
time: 82.8 us; the launch traced here: 82.7 us
  Pallas kernels  79.4 us (96%)
  local copies, waits for them, and re-layouts  2.59 us (3%)
    pallas_call x1, Pallas kernels, on_device(): pl.pallas_call(kernel, out_shape=results, in_specs=[hbm] * 5, out_specs=[...  79.4 us
    unnamed x3, local copies, waits for them, and re-layouts  2.02 us

profile of v3, /device:TPU:6, one launch (start us, length us, event | category | flops | bytes accessed | tf_op | source)
XLA Modules:
  0.0 82.7 jit_solution(2750784926509454025)
XLA Ops:
  0.6 79.4 %bottleneck.1 = (bf16[35,7,256]{2,1,0:T(8,128)(2,1)S(1)}, bf16[35,7,512]{2,1,0:T(8,128)(2,1)S(1)}, bf16[256,256]{1,0:T(8,128)(2,1)S(1)}, f32[2,256]{1,0:T(2,128)S(1)}) custom-call(bf16[5,7,2,14,512]{4,3,2,1,0:T(8,128)(2,1)} %bitcast.10, bf16[4096,256]{1,0:T(8,128)(2,1)} %bitcast.9, f32[1,256]{1,0:T(1,128)} %gain_hbm.1, f32[1,256]{1,0:T(1,128)} %shift_hbm.1, ...), custom_call_target="tpu_custom_call" | custom-call | tf_op jit(solution)/shard_map/bottleneck/pallas_call | solution.py:433
  80.1 0.6 fusion
  80.6 0.7 copy.13
  81.3 0.7 copy.14
  82.0 0.7 copy.15

commit v4 on v3

--- a/solution.py
+++ b/solution.py
@@ -20,6 +20,7 @@
 COPIES = 160
 FAR_FIRST = (8, 7, 9, 6, 10, 5, 11, 4, 12, 3, 13, 2, 14, 1, 15)
 BAND = 64
+CUTS = ((0, 128), (128, 256))
 PARTS = 4
 VMEM_BYTES = 40 * 2**20
 
@@ -44,9 +45,9 @@
 def kernel(
     acts, weight, gain_hbm, shift_hbm, cotan,
     block_out, grad_input, grad_weight, grads,
-    raw, strips, w, gain_ref, shift_ref, ct_raw, ct_strips, pick, own, full, ex, own_rows, mine, gh, hid, cot, acted,
+    raw, strips, w, gain_ref, shift_ref, ct_raw, ct_strips, pick, own, full, ex, own_rows, mine, across, hid, cot, acted,
     stat, grad,
-    to_sib, from_sib, xb, x_opp, x_left, x_right,
+    w_mate, mate, xb, x_opp, x_left, x_right,
     zb, z_opp, z_left, z_right, share, returned,
     send_sems, recv_sems, local_sems, met_sem,
 ):
@@ -271,6 +272,9 @@
 
     tell(stat, mean, square, k_stat)
     along_x()
+    k_w = names(RING)
+    for xx in range(RING):
+        send(w.at[pl.ds(pl.multiple_of(CH * (2 * xx + 1 - core), CH), CH), :], w_mate.at[xx], k_w[xx], sibling)
     keep = pltpu.make_async_copy(
         full.at[:, lax.div(y, 2), :, pl.ds(pl.multiple_of(COLS * lax.rem(y, 2), COLS), COLS)],
         own_rows, local_sems.at[3],
@@ -307,43 +311,35 @@
 
     halves = [pl.ds(0, HALF), pl.ds(HALF, HALF)]
 
-    k_up, k_down, k_far = names(4), names(4), names(4)
+    k_y = [names(RING) for _ in CUTS]
     order = (2, 1, 3, 0)
 
-    def gh_rows(j, r, h):
-        return gh.at[j, pl.ds(PAD * r + HALF * h, HALF), :]
-
-    for j in range(2):
-        gh[j, 0:PAD, :] = mine[:, HALF * j : HALF * (j + 1)]
-        for h in range(2):
-            send(gh_rows(j, 0, h), gh_rows(j, 3, h), k_up[2 * j + h], at_y[1])
-            send(gh_rows(j, 0, 1 - h), gh_rows(j, 1, 1 - h), k_down[2 * j + 1 - h], at_y[3])
-
-    k_cs = [names(4), names(4)]
+    def across_from(j, r):
+        return across.at[pl.ds(CUTS[j][0], CUTS[j][1] - CUTS[j][0]), pl.ds(PAD * r, PAD)]
+
+    k_mate = names(2)
     for q in range(2):
-        for o in order:
-            part = dot(mine[halves[q], :], w_block(around(x, o), 1 - core), (1, 1))
-            to_sib[q, o] = part.astype(BF16)
-            send(to_sib.at[q, o], from_sib.at[q, o], k_cs[q][o], sibling)
+        send(mine.at[halves[q]], mate.at[halves[q]], k_mate[q], sibling)
+    across[:, 0:PAD] = mine[...].T
+    for j in range(len(CUTS)):
+        for o in (2, 1, 3):
+            send(across_from(j, 0), across_from(j, RING - o), k_y[j][o], at_y[o])
 
     last_x()
-    for j in range(2):
-        arrive(gh_rows(j, 3, 0), k_up[2 * j])
-        send(gh_rows(j, 3, 0), gh_rows(j, 2, 0), k_far[2 * j], at_y[1])
-        arrive(gh_rows(j, 1, 1), k_down[2 * j + 1])
-        send(gh_rows(j, 1, 1), gh_rows(j, 2, 1), k_far[2 * j + 1], at_y[3])
-
-    def ring_start(block, opp, left, right, to, ks):
-        mid = block.shape[1] // 2
-        lo, hi = pl.ds(0, mid), pl.ds(mid, mid)
+
+    def ring_start(block, opp, left, right, to, ks, cut, make):
+        lo, hi = pl.ds(cut[0], (cut[1] - cut[0]) // 2), pl.ds((cut[0] + cut[1]) // 2, (cut[1] - cut[0]) // 2)
+        make(2)
         send(block.at[2, lo], opp.at[lo], ks[0], to[1])
         send(block.at[2, hi], opp.at[hi], ks[1], to[3])
+        make(1)
         send(block.at[1, hi], left.at[hi], ks[2], to[1])
+        make(3)
         send(block.at[3, lo], right.at[lo], ks[3], to[3])
-
-    def ring_middle(block, opp, left, right, to, ks):
-        mid = block.shape[1] // 2
-        lo, hi = pl.ds(0, mid), pl.ds(mid, mid)
+        make(0)
+
+    def ring_middle(block, opp, left, right, to, ks, cut):
+        lo, hi = pl.ds(cut[0], (cut[1] - cut[0]) // 2), pl.ds((cut[0] + cut[1]) // 2, (cut[1] - cut[0]) // 2)
         arrive(opp.at[lo], ks[0])
         block[1, lo] = (block[1, lo].astype(F32) + opp[lo].astype(F32)).astype(BF16)
         send(block.at[1, lo], left.at[lo], ks[4], to[1])
@@ -351,70 +347,71 @@
         block[3, hi] = (block[3, hi].astype(F32) + opp[hi].astype(F32)).astype(BF16)
         send(block.at[3, hi], right.at[hi], ks[5], to[3])
 
-    def ring_end(block, left, right, ks):
-        mid = block.shape[1] // 2
-        lo, hi = pl.ds(0, mid), pl.ds(mid, mid)
+    def ring_end(block, left, right, ks, cut):
+        lo, hi = pl.ds(cut[0], (cut[1] - cut[0]) // 2), pl.ds((cut[0] + cut[1]) // 2, (cut[1] - cut[0]) // 2)
         arrive(left.at[hi], ks[2])
         arrive(right.at[lo], ks[3])
         arrive(left.at[lo], ks[4])
         arrive(right.at[hi], ks[5])
-        return block[0].astype(F32) + left[...].astype(F32) + right[...].astype(F32)
-
-    k_x, k_z, k_back = [names(6), names(6)], [names(6), names(6)], names(2)
-    ring_x = [[ref.at[q] for ref in (xb, x_opp, x_left, x_right)] for q in range(2)]
-    ring_z = [[ref.at[j] for ref in (zb, z_opp, z_left, z_right)] for j in range(2)]
+        rows = slice(*cut)
+        return block[0, rows].astype(F32) + left[rows].astype(F32) + right[rows].astype(F32)
+
+    k_x, k_z, k_back = [names(6), names(6)], [names(6) for _ in CUTS], names(2)
+    ring_x = (xb, x_opp, x_left, x_right, at_x)
+    ring_z = (zb, z_opp, z_left, z_right, at_z)
+    cut_x = ((0, HALF), (HALF, PAD))
 
     def start_x(q):
-        for o in order:
+        def make(o):
             part = dot(mine[halves[q], :], w_block(around(x, o), core), (1, 1))
-            arrive(from_sib.at[q, o], k_cs[q][o])
-            xb[q, o] = (part + from_sib[q, o].astype(F32)).astype(BF16)
-        ring_start(*ring_x[q], at_x, k_x[q])
+            part += dot(mate[halves[q], :], w_mate[around(x, o)], (1, 1))
+            xb[o, halves[q]] = part.astype(BF16)
+
+        arrive(mate.at[halves[q]], k_mate[q])
+        ring_start(*ring_x, k_x[q], cut_x[q], make)
 
     def start_z(j):
-        arrive(gh_rows(j, 3, 1), k_up[2 * j + 1])
-        arrive(gh_rows(j, 1, 0), k_down[2 * j])
-        arrive(gh_rows(j, 2, 0), k_far[2 * j])
-        arrive(gh_rows(j, 2, 1), k_far[2 * j + 1])
-        across = gh[j].T
-        for o in order:
+        for o in range(1, RING):
+            arrive(across_from(j, RING - o), k_y[j][o])
+        rows = slice(*CUTS[j])
+
+        def make(o):
             slot = around(zh, o)
             rest = ex[slot, 1:RING].reshape((RING - 1) * PAD, COLS)
-            block = dot(across[:, 0:PAD], own_rows[slot], (1, 0))
-            zb[j, o] = (block + dot(across[:, PAD:], rest, (1, 0))).astype(BF16)
-        ring_start(*ring_z[j], at_z, k_z[j])
+            block = dot(across[rows, 0:PAD], own_rows[slot], (1, 0))
+            zb[o, rows] = (block + dot(across[rows, PAD:], rest, (1, 0))).astype(BF16)
+
+        ring_start(*ring_z, k_z[j], CUTS[j], make)
 
     def give_back(q):
-        block, _, left, right = ring_x[q]
-        share[halves[q], :] = ring_end(block, left, right, k_x[q]).astype(BF16)
+        share[halves[q], :] = ring_end(xb, x_left, x_right, k_x[q], cut_x[q]).astype(BF16)
         send(share.at[halves[q]], returned.at[halves[q]], k_back[q], partner)
 
+    for xx in range(RING):
+        arrive(w_mate.at[xx], k_w[xx])
     start_x(0)
+    spaced = dot(pick[...], acted[...], (1, 0)).reshape(STRIPS, TILE, COLS)
+    block_out[...] = spaced[:, 0:7, :].astype(BF16)
+    grads[...] = sums
+
     keep.wait()
     for i, xx in enumerate((x, lx, rx, ox)):
         arrive(others_of(xx, 1 - core), k_es[i])
     start_z(0)
+    start_z(1)
     start_x(1)
-    start_z(1)
-
-    spaced = dot(pick[...], acted[...], (1, 0)).reshape(STRIPS, TILE, COLS)
-    block_out[...] = spaced[:, 0:7, :].astype(BF16)
-    grads[...] = sums
-
-    ring_middle(*ring_x[0], at_x, k_x[0])
-    ring_middle(*ring_z[0], at_z, k_z[0])
-    ring_middle(*ring_x[1], at_x, k_x[1])
+    ring_middle(*ring_x, k_x[0], cut_x[0])
+    ring_middle(*ring_x, k_x[1], cut_x[1])
+    ring_middle(*ring_z, k_z[0], CUTS[0])
     give_back(0)
-    ring_middle(*ring_z[1], at_z, k_z[1])
+    ring_middle(*ring_z, k_z[1], CUTS[1])
     give_back(1)
-    for j in range(2):
-        block, _, left, right = ring_z[j]
-        grad_weight[:, HALF * j : HALF * (j + 1)] = ring_end(block, left, right, k_z[j]).T.astype(BF16)
-
     for q in range(2):
         arrive(returned.at[halves[q]], k_back[q])
     spaced = dot(pick[...], returned[...], (1, 0)).reshape(STRIPS, TILE, CH)
     grad_input[...] = spaced[:, 0:7, :].astype(BF16)
+    for j in range(2):
+        grad_weight[:, halves[j]] = ring_end(zb, z_left, z_right, k_z[j], CUTS[j]).T.astype(BF16)
     for copy in started:
         copy.wait_send()
 
@@ -449,22 +446,22 @@
             pltpu.VMEM((RING, RING, 2, HALF, COLS), BF16),
             pltpu.VMEM((RING, PAD, COLS), BF16),
             pltpu.VMEM((PAD, COLS), BF16),
-            pltpu.VMEM((2, RING * PAD, HALF), BF16),
+            pltpu.VMEM((COLS, RING * PAD), BF16),
             pltpu.VMEM((PAD, COLS), F32),
             pltpu.VMEM((PAD, COLS), F32),
             pltpu.VMEM((PAD, COLS), BF16),
             pltpu.VMEM((RING * RING, 2, COLS), F32),
             pltpu.VMEM((RING * RING, 2, COLS), F32),
-            pltpu.VMEM((2, RING, HALF, CH), BF16),
-            pltpu.VMEM((2, RING, HALF, CH), BF16),
-            pltpu.VMEM((2, RING, HALF, CH), BF16),
-            pltpu.VMEM((2, HALF, CH), BF16),
-            pltpu.VMEM((2, HALF, CH), BF16),
-            pltpu.VMEM((2, HALF, CH), BF16),
-            pltpu.VMEM((2, RING, HALF, COLS), BF16),
-            pltpu.VMEM((2, HALF, COLS), BF16),
-            pltpu.VMEM((2, HALF, COLS), BF16),
-            pltpu.VMEM((2, HALF, COLS), BF16),
+            pltpu.VMEM((RING, CH, COLS), BF16),
+            pltpu.VMEM((PAD, COLS), BF16),
+            pltpu.VMEM((RING, PAD, CH), BF16),
+            pltpu.VMEM((PAD, CH), BF16),
+            pltpu.VMEM((PAD, CH), BF16),
+            pltpu.VMEM((PAD, CH), BF16),
+            pltpu.VMEM((RING, COLS, COLS), BF16),
+            pltpu.VMEM((COLS, COLS), BF16),
+            pltpu.VMEM((COLS, COLS), BF16),
+            pltpu.VMEM((COLS, COLS), BF16),
             pltpu.VMEM((PAD, CH), BF16),
             pltpu.VMEM((PAD, CH), BF16),
             pltpu.SemaphoreType.DMA((COPIES,)),

time: 82.8 us -> 81.3 us (0.982)
  Pallas kernels: 79.4 us -> 77.9 us
    pallas_call x1, Pallas kernels: 79.4 us -> 77.9 us  [on_device(): pl.pallas_call(kernel, out_shape=results, in_specs=[hbm] * 5, out_specs=[...]
where the time goes in v4:
time: 81.3 us; the launch traced here: 81.1 us
  Pallas kernels  77.9 us (96%)
  local copies, waits for them, and re-layouts  2.59 us (3%)
    pallas_call x1, Pallas kernels, on_device(): pl.pallas_call(kernel, out_shape=results, in_specs=[hbm] * 5, out_specs=[...  77.9 us
    unnamed x3, local copies, waits for them, and re-layouts  2.02 us

profile of v4, /device:TPU:6, one launch (start us, length us, event | category | flops | bytes accessed | tf_op | source)
XLA Modules:
  0.0 81.1 jit_solution(3910133706043828344)
XLA Ops:
  0.6 77.9 %bottleneck.1 = (bf16[35,7,256]{2,1,0:T(8,128)(2,1)S(1)}, bf16[35,7,512]{2,1,0:T(8,128)(2,1)S(1)}, bf16[256,256]{1,0:T(8,128)(2,1)S(1)}, f32[2,256]{1,0:T(2,128)S(1)}) custom-call(bf16[5,7,2,14,512]{4,3,2,1,0:T(8,128)(2,1)} %bitcast.10, bf16[4096,256]{1,0:T(8,128)(2,1)} %bitcast.9, f32[1,256]{1,0:T(1,128)} %gain_hbm.1, f32[1,256]{1,0:T(1,128)} %shift_hbm.1, ...), custom_call_target="tpu_custom_call" | custom-call | tf_op jit(solution)/shard_map/bottleneck/pallas_call | solution.py:430
  78.5 0.6 fusion
  79.1 0.7 copy.13
  79.8 0.7 copy.14
  80.5 0.7 copy.15

commit v5 on v4

--- a/solution.py
+++ b/solution.py
@@ -17,11 +17,11 @@
 COLS = 256
 TILE = 16
 STRIPS = 35
-COPIES = 160
+COPIES = 192
 FAR_FIRST = (8, 7, 9, 6, 10, 5, 11, 4, 12, 3, 13, 2, 14, 1, 15)
 BAND = 64
 CUTS = ((0, 128), (128, 256))
-PARTS = 4
+PARTS = 8
 VMEM_BYTES = 40 * 2**20
 
 

time: 81.3 us -> 80.9 us (level)
  no operation moved by 1% of the time
where the time goes in v5:
time: 80.9 us; the launch traced here: 80.8 us
  Pallas kernels  77.5 us (96%)
  local copies, waits for them, and re-layouts  2.59 us (3%)
    pallas_call x1, Pallas kernels, on_device(): pl.pallas_call(kernel, out_shape=results, in_specs=[hbm] * 5, out_specs=[...  77.5 us
    unnamed x3, local copies, waits for them, and re-layouts  2.02 us

profile of v5, /device:TPU:6, one launch (start us, length us, event | category | flops | bytes accessed | tf_op | source)
XLA Modules:
  0.0 80.8 jit_solution(15969429231760533757)
XLA Ops:
  0.6 77.5 %bottleneck.1 = (bf16[35,7,256]{2,1,0:T(8,128)(2,1)S(1)}, bf16[35,7,512]{2,1,0:T(8,128)(2,1)S(1)}, bf16[256,256]{1,0:T(8,128)(2,1)S(1)}, f32[2,256]{1,0:T(2,128)S(1)}) custom-call(bf16[5,7,2,14,512]{4,3,2,1,0:T(8,128)(2,1)} %bitcast.10, bf16[4096,256]{1,0:T(8,128)(2,1)} %bitcast.9, f32[1,256]{1,0:T(1,128)} %gain_hbm.1, f32[1,256]{1,0:T(1,128)} %shift_hbm.1, ...), custom_call_target="tpu_custom_call" | custom-call | tf_op jit(solution)/shard_map/bottleneck/pallas_call | solution.py:430
  78.2 0.6 fusion
  78.7 0.7 copy.13
  79.4 0.7 copy.14
  80.1 0.7 copy.15
